TPU v7x, 256 devices: a whole 4x4x8 slice. The times are simulated.
256 devices in a mesh: row: 8 (over x, core), col: 32 (over y, z).
Axes of the slice: x: 4, y: 4, z: 8, core: 2. Of those that a mesh axis runs over, the one named last changes fastest.
Arguments:
- src_emb: bfloat16 [4096, 1024], P('row', 'col'), may hold values from -6 to 6
- tgt_emb: bfloat16 [16384, 1024], P('col', 'row'), may hold values from -8.5 to 8.5
- rotation: bfloat16 [1024, 1024], replicated, may hold values from -1.1 to 1.1
- src_ids: int32 [4096], P('row'), may hold values from 0 to 99999
- tgt_ids: int32 [16384], P('col'), may hold values from 0 to 99999
Outputs:
- polar_step: float32 [1024, 1024], P(('row', 'col'))
All inputs are finite; a program needn't handle non-finite values.
Results may differ from a plain program's by a relative error of at most 0.01.
Values may be sent and summed in bfloat16 or wider, within the bound.
A program may use at most 64 MiB of HBM per device.

v0:
```python
import math

import jax
import jax.numpy as jnp
from jax import lax
from jax.sharding import PartitionSpec as P

D = 1024
ITERS = 3


def unit_rows(emb):
    values = emb.astype(jnp.float32)
    scale = lax.rsqrt(jnp.mean(values * values, axis=1, keepdims=True) + 1e-06) / math.sqrt(D)
    return (values * scale).astype(jnp.bfloat16)


def shards(src_emb, tgt_emb, rotation, src_ids, tgt_ids):
    src_unit = unit_rows(lax.all_gather(src_emb, "col", axis=1, tiled=True))
    tgt_unit = unit_rows(lax.all_gather(tgt_emb, "row", axis=1, tiled=True))
    rotated = jnp.dot(src_unit, rotation, preferred_element_type=jnp.float32).astype(jnp.bfloat16)
    kernel = jnp.exp(jnp.dot(rotated, tgt_unit.T, preferred_element_type=jnp.float32) / 0.03)
    src_mass = lax.rsqrt(1000.0 + src_ids.astype(jnp.float32))
    tgt_mass = lax.rsqrt(1000.0 + tgt_ids.astype(jnp.float32))
    tgt_scale = jnp.ones((kernel.shape[1],), jnp.float32)
    for step in range(ITERS):
        row_part = jnp.dot(kernel, tgt_scale, precision=lax.Precision.HIGHEST)
        src_scale = src_mass / lax.psum(row_part, "col")
        col_part = jnp.dot(src_scale, kernel, precision=lax.Precision.HIGHEST)
        tgt_scale = tgt_mass / lax.psum(col_part, "row")
    plan = (src_scale[:, None] * kernel * tgt_scale[None, :]).astype(jnp.bfloat16)
    carried = jnp.dot(plan, tgt_unit, preferred_element_type=jnp.float32).astype(jnp.bfloat16)
    width = src_unit.shape[1]
    devices = lax.axis_size(("row", "col"))
    share = width // devices
    term = lax.dot_general(
        src_unit, carried, (((0,), (0,)), ((), ())), preferred_element_type=jnp.float32
    )
    cross = lax.psum(term, ("row", "col"))
    normed = cross * lax.rsqrt(jnp.mean(cross * cross) + 1e-30) / (2.0 * math.sqrt(width))
    first = lax.axis_index(("row", "col")) * share
    mine = lax.dynamic_slice_in_dim(normed, first, share, 0)
    gram_rows = jnp.dot(mine, normed.T, precision=lax.Precision.HIGHEST)
    cubic = jnp.dot(gram_rows, normed, precision=lax.Precision.HIGHEST)
    return math.sqrt(width) * (1.5 * mine - 0.5 * cubic)


def solution(mesh):
    return jax.shard_map(
        shards,
        mesh=mesh,
        in_specs=(P("row", "col"), P("col", "row"), P(), P("row"), P("col")),
        out_specs=P(("row", "col"), None),
        check_vma=False,
    )
```

profile of v0, /device:TPU:1, one launch (start us, length us, event | category | flops | bytes accessed | tf_op | source)
XLA Modules:
  0.0 662.8 jit_solution(6076874470653943615)
XLA Ops:
  6.5 0.7 all-gather.5.cloned.1.call-update
  7.3 0.0 all-gather.3.cloned.1.call-start
  7.3 0.7 all-gather.3.cloned.1.call-update
  8.0 0.0 all-reduce.2.cloned.1.call-start
  8.1 31.3 %all-gather.5.cloned.1.call-done = bf16[512,1024]{1,0:T(8,128)(2,1)} async-done(((bf16[512,128]{1,0:T(8,128)(2,1)}), bf16[512,1024]{1,0:T(8,128)(2,1)}) %all-gather.5.cloned.1.call-update) | async-done | bytes 1048592 | tf_op jit(solution)/shard_map/all_gather | solution.py:20
  39.3 1.5 fusion.2
  40.8 73.5 %all-gather.3.cloned.1.call-done = bf16[512,1024]{0,1:T(8,128)(2,1)} async-done(((bf16[512,32]{0,1:T(8,128)(2,1)}), bf16[512,1024]{0,1:T(8,128)(2,1)}) %all-gather.3.cloned.1.call-update) | async-done | bytes 1048592 | tf_op jit(solution)/shard_map/all_gather | solution.py:19
  114.3 1.5 fusion
  115.8 0.0 copy-start.1
  115.8 3.4 fusion.4
  119.2 0.0 copy-start.2
  119.2 1.0 fusion.26
  120.2 58.2 %psum.49 = f32[512]{0:T(512)S(1)} all-reduce(f32[512]{0:T(512)S(1)} %bitcast.35), channel_id=1, replica_groups=mesh['row'=8,'col'=32] {'col'}, use_global_device_ids=true, to_apply=%region_2.0 | all-reduce | flops 512 | bytes 4096 | tf_op jit(solution)/shard_map/psum | solution.py:28
  178.4 0.0 copy-done.1
  178.4 0.6 fusion.30
  179.0 30.9 %psum.50 = f32[512]{0:T(512)S(1)} all-reduce(f32[512]{0:T(512)S(1)} %bitcast.31), channel_id=1, replica_groups=mesh['row'=8,'col'=32] {'row'}, use_global_device_ids=true, to_apply=%region_3.0 | all-reduce | flops 512 | bytes 4096 | tf_op jit(solution)/shard_map/psum | solution.py:30
  209.9 0.0 copy-done.2
  209.9 1.0 fusion.31
  210.9 55.7 %psum.51 = f32[512]{0:T(512)S(1)} all-reduce(f32[512]{0:T(512)S(1)} %bitcast.32), channel_id=1, replica_groups=mesh['row'=8,'col'=32] {'col'}, use_global_device_ids=true, to_apply=%region_4.0 | all-reduce | flops 512 | bytes 4096 | tf_op jit(solution)/shard_map/psum | solution.py:28
  266.7 0.6 fusion.32
  267.3 26.3 %psum.52 = f32[512]{0:T(512)S(1)} all-reduce(f32[512]{0:T(512)S(1)} %bitcast.33), channel_id=1, replica_groups=mesh['row'=8,'col'=32] {'row'}, use_global_device_ids=true, to_apply=%region_5.0 | all-reduce | flops 512 | bytes 4096 | tf_op jit(solution)/shard_map/psum | solution.py:30
  293.6 1.0 fusion.33
  294.6 57.4 %psum.53 = f32[512]{0:T(512)S(1)} all-reduce(f32[512]{0:T(512)S(1)} %bitcast.34), channel_id=1, replica_groups=mesh['row'=8,'col'=32] {'col'}, use_global_device_ids=true, to_apply=%region_6.0 | all-reduce | flops 512 | bytes 4096 | tf_op jit(solution)/shard_map/psum | solution.py:28
  352.0 0.6 fusion.34
  352.6 26.8 %psum.54 = f32[512]{0:T(512)S(1)} all-reduce(f32[512]{0:T(512)S(1)} %bitcast.36), channel_id=1, replica_groups=mesh['row'=8,'col'=32] {'row'}, use_global_device_ids=true, to_apply=%region_7.0 | all-reduce | flops 512 | bytes 4096 | tf_op jit(solution)/shard_map/psum | solution.py:30
  379.4 5.4 fusion.5
  384.8 0.0 all-reduce.2.cloned.1.call-update
  384.8 257.9 %all-reduce.2.cloned.1.call-done = f32[1024,1024]{1,0:T(8,128)} async-done(((f32[1024,1024]{1,0:T(8,128)}), f32[1024,1024]{1,0:T(8,128)}) %all-reduce.2.cloned.1.call-update) | async-done | bytes 4194320 | tf_op jit(solution)/shard_map/psum | solution.py:39
  642.8 3.9 multiply_reduce_fusion
  647.4 2.7 multiply_multiply_fusion
  650.0 3.5 fusion.18
  653.6 2.7 fusion.7
  (11 shorter events, 0.1 us)
Async XLA Ops:
  6.5 109.3 %copy-start = (bf16[1024,1024]{1,0:T(8,128)(2,1)S(1)}, bf16[1024,1024]{1,0:T(8,128)(2,1)}, u32[]{:S(2)}) copy-start(bf16[1024,1024]{1,0:T(8,128)(2,1)} %param.7) | copy-start | bytes 6291460
  6.5 32.8 %all-gather.5.cloned.1.call-start = ((), (), s32[]{:S(2)}) async-start(), calls=%async_computation.1 | async-start | bytes 1179648 | tf_op jit(solution)/shard_map/all_gather | solution.py:20
  7.3 107.1 %all-gather.3.cloned.1.call-start = ((), (), s32[]{:S(2)}) async-start(), calls=%async_computation | async-start | bytes 1081344 | tf_op jit(solution)/shard_map/all_gather | solution.py:19
  8.0 634.8 %all-reduce.2.cloned.1.call-start = ((), (), s32[]{:S(2)}) async-start(), calls=%async_computation.2 | async-start | bytes 8388608 | tf_op jit(solution)/shard_map/psum | solution.py:39
  115.8 62.6 %copy-start.1 = (s32[512]{0:T(512)S(1)}, s32[512]{0:T(512)}, u32[]{:S(2)}) copy-start(s32[512]{0:T(512)} %param.8) | copy-start | bytes 6148
  119.2 90.7 %copy-start.2 = (s32[512]{0:T(512)S(1)}, s32[512]{0:T(512)}, u32[]{:S(2)}) copy-start(s32[512]{0:T(512)} %param.9) | copy-start | bytes 6148
Sparse Core Ops, SparseCore 0:
  9.2 30.0 all-gather.4
  41.9 72.3 all-gather.2
  385.0 257.7 all-reduce.1
where the time goes:
time: 664 us; the launch traced here: 663 us
  waiting for transfers between devices  364 us (55%)
  blocking collectives  255 us (38%)
  matrix products  19.7 us (3%)
  between operations  13.9 us (2%)
  other arithmetic  9.62 us (1%)
    psum x1, waiting for transfers between devices, shards(): cross = lax.psum(term, ('row', 'col'))  258 us
    psum x3, blocking collectives, shards(): src_scale = src_mass / lax.psum(row_part, 'col')  171 us
    psum x3, blocking collectives, shards(): tgt_scale = tgt_mass / lax.psum(col_part, 'row')  84 us
    all_gather x1, waiting for transfers between devices, shards(): src_unit = unit_rows(lax.all_gather(src_emb, 'col', axis=1, tiled=True))  73.5 us
    all_gather x1, waiting for transfers between devices, shards(): tgt_unit = unit_rows(lax.all_gather(tgt_emb, 'row', axis=1, tiled=True))  31.3 us
  transfers between devices with their start and end apart: 3, of which 3 were waited for; matrix products, arithmetic and copies ran while one was open for 0% of the time, Pallas kernels for 0%

commit v1 on v0

v1 whole, which is shorter than its diff:
```python
import math

import jax
import jax.numpy as jnp
from jax import lax
from jax.experimental import pallas as pl
from jax.experimental.pallas import tpu as pltpu
from jax.sharding import PartitionSpec as P

MESH = pl.DeviceIdType.MESH
F32 = jnp.float32
BF16 = jnp.bfloat16
D = 1024
W = 512
ITERS = 3
X, Y, Z = 4, 4, 8
ROWS, COLS = 2 * X, Y * Z
NN = (((1,), (0,)), ((), ()))
NT = (((1,), (1,)), ((), ()))


def dot(a, b, dims):
    return lax.dot_general(a, b, dims, preferred_element_type=F32)


def send(src, dst, send_sem, recv_sem, device):
    pltpu.make_async_remote_copy(
        src_ref=src, dst_ref=dst, send_sem=send_sem, recv_sem=recv_sem,
        device_id=device, device_id_type=MESH,
    ).start()


def wait(ref, sem):
    pltpu.make_async_copy(ref, ref, sem).wait()


def block(i, size):
    return pl.ds(pl.multiple_of(i * size, size), size)


def body(src_hbm, tgt_hbm, rot_hbm, src_ids, tgt_ids, out_ref,
         src_v, src_t, tgt, rot, u, kt, colbuf, rowbuf,
         a_mine, a_mate, a_x, a_out, yb, y_out, zb, z_out, xf,
         local, zs, xs, ss, rs):
    r, c = lax.axis_index("row"), lax.axis_index("col")
    x, core = r // 2, r % 2
    y, z = c // Z, c % Z
    mate = (2 * x + (1 - core), c)

    def xpeer(k):
        return (2 * ((x + k) % X) + core, c)

    def ypeer(k):
        return (r, Z * ((y + k) % Y) + z)

    def zpeer(k):
        return (r, Z * y + (z + k) % Z)

    def colpeer(k):
        return (r, (c + k) % COLS)

    def rowpeer(k):
        return ((r + k) % ROWS, c)

    load_src = pltpu.make_async_copy(src_hbm, src_v, local.at[0])
    load_src.start()
    my_tgt = tgt.at[:, block(r, 128)]
    load_tgt = pltpu.make_async_copy(tgt_hbm, my_tgt, local.at[1])
    load_tgt.start()
    load_rot = pltpu.make_async_copy(rot_hbm, rot, local.at[2])
    load_rot.start()
    bar = pltpu.get_barrier_semaphore()

    def greet_col(k, _):
        pl.semaphore_signal(bar, inc=1, device_id=colpeer(k), device_id_type=MESH)
        return 0

    def greet_row(k, _):
        pl.semaphore_signal(bar, inc=1, device_id=rowpeer(k), device_id_type=MESH)
        return 0

    lax.fori_loop(1, COLS, greet_col, 0)
    lax.fori_loop(1, ROWS, greet_row, 0)
    load_src.wait()
    eye = (lax.broadcasted_iota(jnp.int32, (32, 32), 0)
           == lax.broadcasted_iota(jnp.int32, (32, 32), 1)).astype(BF16)
    src_t[block(c, 32), :] = dot(eye, src_v[...], NT).astype(BF16)
    load_tgt.wait()
    pl.semaphore_wait(bar, COLS + ROWS - 2)

    mine = src_t.at[block(c, 32), :]
    for k in (1, 7, 2, 6, 3, 5, 4):
        send(mine, mine, ss.at[0], zs.at[k], zpeer(k))
    for k in (1, 3, 2):
        send(my_tgt, my_tgt, ss.at[1], xs.at[k], xpeer(k))
        send(mine, mine, ss.at[2], rs.at[2], ypeer(k))
    send(my_tgt, my_tgt, ss.at[3], rs.at[3], mate)

    def forward_src(k):
        got = src_t.at[block(Z * y + (z + Z - k) % Z, 32), :]
        wait(got, zs.at[k])
        for j in (1, 3, 2):
            send(got, got, ss.at[2], rs.at[2], ypeer(j))

    def forward_tgt(k):
        got = tgt.at[:, block(2 * ((x + X - k) % X) + core, 128)]
        wait(got, xs.at[k])
        send(got, got, ss.at[3], rs.at[3], mate)

    forward_src(1)
    forward_src(7)
    forward_tgt(1)
    forward_tgt(3)
    forward_src(2)
    forward_src(6)
    forward_tgt(2)
    forward_src(3)
    forward_src(5)
    forward_src(4)

    wait(tgt.at[:, pl.ds(0, 512)], rs.at[3])
    load_rot.wait()
    tv = tgt[...].astype(F32)
    tsum = jnp.sum(tv * tv, axis=1, keepdims=True)
    tscale = lax.rsqrt(tsum * (1.0 / D) + 1e-06) * (1.0 / math.sqrt(D))
    u[...] = (dot(tgt[...], rot[...], NT) * tscale).astype(BF16)
    tscale_l = jnp.transpose(jnp.broadcast_to(tscale, (W, 128)))[0:1, :]
    src_mass = lax.rsqrt(1000.0 + src_ids[...].astype(F32))
    tgt_mass = lax.rsqrt(1000.0 + tgt_ids[...].astype(F32))

    wait(src_t.at[pl.ds(0, 24 * 32), :], rs.at[2])
    sv = src_t[...].astype(F32)
    ssum = jnp.sum(sv * sv, axis=0, keepdims=True)
    sscale = lax.rsqrt(ssum * (1.0 / D) + 1e-06) * (1.0 / math.sqrt(D))
    kt[...] = jnp.exp(dot(u[...], src_t[...], NN) * (sscale * (1.0 / 0.03))).astype(BF16)

    row8 = lax.broadcasted_iota(jnp.int32, (8, W), 0)

    def matvec(v, dims):
        high = v.astype(BF16).astype(F32)
        both = jnp.where(row8 == 0, high, jnp.where(row8 == 1, v - high, 0.0)).astype(BF16)
        return jnp.sum(dot(both, kt[...], dims), axis=0, keepdims=True)

    def sum_col(part, it):
        colbuf[it, c] = part

        def one(k, _):
            send(colbuf.at[it, c], colbuf.at[it, c], ss.at[4 + it], rs.at[4 + it], colpeer(k))
            return 0

        lax.fori_loop(1, COLS, one, 0)
        wait(colbuf.at[it, pl.ds(0, COLS - 1)], rs.at[4 + it])
        return jnp.sum(colbuf[it], axis=0)

    def start_row(part, it):
        rowbuf[it, r] = part
        for k in range(1, ROWS):
            send(rowbuf.at[it, r], rowbuf.at[it, r], ss.at[7 + it], rs.at[7 + it], rowpeer(k))

    def end_row(it):
        wait(rowbuf.at[it, pl.ds(0, ROWS - 1)], rs.at[7 + it])
        return jnp.sum(rowbuf[it], axis=0)

    tgt_scale = jnp.ones((1, W), F32)
    for it in range(ITERS):
        src_scale = src_mass / sum_col(matvec(tgt_scale, NN), it)
        start_row(matvec(src_scale, NT), it)
        if it < ITERS - 1:
            tgt_scale = tgt_mass / end_row(it)

    kt[...] = (kt[...].astype(F32) * (src_scale * sscale)).astype(BF16)
    for j in range(X):
        a_out[j] = dot(src_t[block(2 * j + (1 - core), 128), :], kt[...], NT).astype(BF16)
        send(a_out.at[j], a_mate.at[j], ss.at[10], rs.at[10], mate)
    for j in range(X):
        a_mine[j] = dot(src_t[block(2 * j + core, 128), :], kt[...], NT)
    wait(a_mate, rs.at[10])
    for j in range(X):
        a_out[X + j] = (a_mine[j] + a_mate[j].astype(F32)).astype(BF16)
    for k in (2, 1, 3):
        send(a_out.at[X + (x + k) % X], a_x.at[k - 1], ss.at[11], rs.at[11], xpeer(k))
    tgt_scale = tgt_mass / end_row(ITERS - 1)
    wait(a_x, rs.at[11])
    total = (a_mine[x] + a_mate[x].astype(F32)) + (
        a_x[0].astype(F32) + a_x[1].astype(F32) + a_x[2].astype(F32))
    total = (total * (tgt_scale * tscale_l)).astype(BF16)

    cross = dot(total, tgt[...], NN)
    for j in range(Y):
        y_out[j] = cross[:, 256 * j:256 * (j + 1)].astype(BF16)
    for k in (2, 1, 3):
        send(y_out.at[(y + k) % Y], yb.at[k - 1], ss.at[12], rs.at[12], ypeer(k))
    wait(yb, rs.at[12])
    part = (y_out[y].astype(F32) + yb[0].astype(F32)) + (yb[1].astype(F32) + yb[2].astype(F32))
    z_out[...] = part.astype(BF16).reshape(Z, 16, 256)
    for k in (4, 3, 5, 2, 6, 1, 7):
        send(z_out.at[(z + k) % Z], zb.at[k - 1], ss.at[13], rs.at[13], zpeer(k))
    wait(zb, rs.at[13])
    own = z_out[z].astype(F32) + jnp.sum(zb[...].astype(F32), axis=0)

    def part_ref(row, first, count, col, rows=1):
        return xf.at[pl.ds(pl.multiple_of(row * 128 + first, 16), count),
                     pl.ds(pl.multiple_of(col * 256, 256), 256)]

    xf[pl.ds(pl.multiple_of(r * 128 + z * 16, 16), 16), block(y, 256)] = own.astype(BF16)
    mine = part_ref(r, z * 16, 16, y)
    for k in (4, 3, 5, 2, 6, 1, 7):
        send(mine, mine, ss.at[14], rs.at[14], zpeer(k))
    wait(xf.at[pl.ds(0, 112), pl.ds(0, 256)], rs.at[14])

    first_half, second_half = part_ref(r, 0, 64, y), part_ref(r, 64, 64, y)
    for k in (2, 1, 3):
        send(first_half, first_half, ss.at[15], zs.at[8 + k], xpeer(k))
        send(second_half, second_half, ss.at[16], zs.at[12 + k], ypeer(k))
    for k in (1, 3, 2):
        send(first_half, first_half, ss.at[17], rs.at[17], ypeer(k))
        send(second_half, second_half, ss.at[18], rs.at[18], xpeer(k))
    both = part_ref(r, 0, 128, y)
    send(both, both, ss.at[19], rs.at[19], mate)
    for k in (1, 3, 2):
        got = part_ref(2 * ((x + X - k) % X) + core, 0, 64, y)
        wait(got, zs.at[8 + k])
        for j in (1, 3, 2):
            send(got, got, ss.at[17], rs.at[17], ypeer(j))
        send(got, got, ss.at[19], rs.at[19], mate)
        got = part_ref(r, 64, 64, (y + Y - k) % Y)
        wait(got, zs.at[12 + k])
        for j in (1, 3, 2):
            send(got, got, ss.at[18], rs.at[18], xpeer(j))
        send(got, got, ss.at[19], rs.at[19], mate)
    wait(xf.at[pl.ds(0, 192), :], rs.at[17])
    wait(xf.at[pl.ds(0, 192), :], rs.at[18])
    for k in range(1, X):
        for j in range(1, Y):
            got = part_ref(2 * ((x + k) % X) + core, 0, 64, (y + j) % Y)
            send(got, got, ss.at[19], rs.at[19], mate)
            got = part_ref(2 * ((x + k) % X) + core, 64, 64, (y + j) % Y)
            send(got, got, ss.at[19], rs.at[19], mate)
    for k in range(1, Y):
        got = part_ref(r, 0, 64, (y + k) % Y)
        send(got, got, ss.at[19], rs.at[19], mate)
        got = part_ref(2 * ((x + k) % X) + core, 64, 64, y)
        send(got, got, ss.at[19], rs.at[19], mate)
    wait(xf.at[pl.ds(0, 512), :], rs.at[19])

    pick = (lax.broadcasted_iota(jnp.int32, (8, 128), 1)
            == 4 * c + lax.broadcasted_iota(jnp.int32, (8, 128), 0) % 4).astype(BF16)
    rows = dot(pick, xf[block(r, 128), :], NN)
    full = xf[...].astype(F32)
    mean = jnp.sum(full * full, keepdims=True) * (1.0 / (D * D))
    scale = lax.rsqrt(mean + 1e-30) * (1.0 / (2.0 * math.sqrt(D)))
    gram = dot(rows.astype(BF16), xf[...], NT) * (scale * scale)
    cubic = dot(gram.astype(BF16), xf[...], NN) * scale
    result = math.sqrt(D) * (1.5 * (rows * scale) - 0.5 * cubic)
    out_ref[...] = result[0:4, :]

    wait(src_t.at[pl.ds(0, 224), :], ss.at[0])
    wait(tgt.at[:, pl.ds(0, 384)], ss.at[1])
    wait(src_t.at[pl.ds(0, 768), :], ss.at[2])
    wait(tgt.at[:, pl.ds(0, 512)], ss.at[3])
    for it in range(ITERS):
        wait(colbuf.at[it, pl.ds(0, COLS - 1)], ss.at[4 + it])
        wait(rowbuf.at[it, pl.ds(0, ROWS - 1)], ss.at[7 + it])
    wait(a_mate, ss.at[10])
    wait(a_x, ss.at[11])
    wait(yb, ss.at[12])
    wait(zb, ss.at[13])
    wait(xf.at[pl.ds(0, 112), pl.ds(0, 256)], ss.at[14])
    wait(xf.at[pl.ds(0, 192), pl.ds(0, 256)], ss.at[15])
    wait(xf.at[pl.ds(0, 192), pl.ds(0, 256)], ss.at[16])
    wait(xf.at[pl.ds(0, 192), :], ss.at[17])
    wait(xf.at[pl.ds(0, 192), :], ss.at[18])
    wait(xf.at[pl.ds(0, 512), :], ss.at[19])


def shards(src_emb, tgt_emb, rotation, src_ids, tgt_ids):
    vmem = pltpu.VMEM
    scratch = [
        vmem((W, 32), BF16),
        vmem((D, W), BF16),
        vmem((W, D), BF16),
        vmem((D, D), BF16),
        vmem((W, D), BF16),
        vmem((W, W), BF16),
        vmem((ITERS, COLS, 1, W), F32),
        vmem((ITERS, ROWS, 1, W), F32),
        vmem((X, 128, W), F32),
        vmem((X, 128, W), BF16),
        vmem((X - 1, 128, W), BF16),
        vmem((2 * X, 128, W), BF16),
        vmem((Y - 1, 128, 256), BF16),
        vmem((Y, 128, 256), BF16),
        vmem((Z - 1, 16, 256), BF16),
        vmem((Z, 16, 256), BF16),
        vmem((D, D), BF16),
        pltpu.SemaphoreType.DMA((3,)),
        pltpu.SemaphoreType.DMA((16,)),
        pltpu.SemaphoreType.DMA((4,)),
        pltpu.SemaphoreType.DMA((20,)),
        pltpu.SemaphoreType.DMA((20,)),
    ]
    hbm = pl.BlockSpec(memory_space=pl.ANY)
    here = pl.BlockSpec(memory_space=pltpu.VMEM)
    return pl.pallas_call(
        body,
        out_shape=jax.ShapeDtypeStruct((4, D), F32),
        in_specs=[hbm, hbm, hbm, here, here],
        out_specs=here,
        scratch_shapes=scratch,
        compiler_params=pltpu.CompilerParams(
            collective_id=0, has_side_effects=True, vmem_limit_bytes=48 * 2**20
        ),
        name="procrustes",
    )(src_emb, tgt_emb, rotation, src_ids.reshape(1, W), tgt_ids.reshape(1, W))


def solution(mesh):
    return jax.shard_map(
        shards,
        mesh=mesh,
        in_specs=(P("row", "col"), P("col", "row"), P(), P("row"), P("col")),
        out_specs=P(("row", "col"), None),
        check_vma=False,
    )
```

time: 664 us -> 99.3 us (0.15)
  waiting for transfers between devices: 364 us -> 0 us
  blocking collectives: 255 us -> 0 us
  Pallas kernels: 0 us -> 93.7 us
  matrix products: 19.7 us -> 0 us
  between operations: 13.9 us -> 0.02 us
  other arithmetic: 9.62 us -> 0 us
    psum x1 -> x0, waiting for transfers between devices: 258 us -> none  [shards(): cross = lax.psum(term, ('row', 'col'))]
    psum x6 -> x0, blocking collectives: 255 us -> none  [the longest x3 171 us: shards(): src_scale = src_mass / lax.psum(row_part, 'col')]
    all_gather x2 -> x0, waiting for transfers between devices: 105 us -> none  [the longest x1 73.5 us: shards(): src_unit = unit_rows(lax.all_gather(src_emb, 'col', axis=1, tiled=True))]
    pallas_call x0 -> x1, Pallas kernels: none -> 93.7 us  [shards(): pl.pallas_call(body, out_shape=jax.ShapeDtypeStruct((4, D), F32), in_spec...]
    dot_general x10 -> x0, matrix products: 19.7 us -> none  [the longest x1 5.38 us: shards(): lax.dot_general(src_unit, carried, (((0,), (0,)), ((), ())), preferred_el...]
    reduce_sum x3 -> x0, other arithmetic: 6.87 us -> none  [the longest x1 3.87 us: shards(): jnp.mean(cross * cross) + 1e-30]
  transfers between devices with their start and end apart: 3 -> 0, of which waited for: 3 -> 0; matrix products, arithmetic and copies ran while one was open for 0% -> 0% of each run, Pallas kernels for 0% -> 0%
where the time goes in v1:
time: 99.3 us; the launch traced here: 99.1 us
  Pallas kernels  93.7 us (94%)
  local copies, waits for them, and re-layouts  5.34 us (5%)
    pallas_call x1, Pallas kernels, shards(): pl.pallas_call(body, out_shape=jax.ShapeDtypeStruct((4, D), F32), in_spec...  93.7 us
    unnamed x10, local copies, waits for them, and re-layouts  5.34 us

profile of v1, /device:TPU:1, one launch (start us, length us, event | category | flops | bytes accessed | tf_op | source)
XLA Modules:
  0.0 99.1 jit_solution(8728518767598335370)
XLA Ops:
  0.0 0.9 copy.6.src_hbm
  0.9 0.0 copy-start
  0.9 1.6 %copy-done = bf16[1024,1024]{1,0:T(8,128)(2,1)S(1)} copy-done((bf16[1024,1024]{1,0:T(8,128)(2,1)S(1)}, bf16[1024,1024]{1,0:T(8,128)(2,1)}, u32[]{:S(2)}) %copy-start) | copy-done | bytes 2097176
  2.5 0.0 copy-start.1
  2.5 0.9 copy-done.1
  3.4 0.0 copy-start.2
  3.4 0.7 copy-done.2
  4.1 0.0 copy-start.3
  4.1 0.7 copy-done.3
  4.7 93.7 %procrustes.1 = f32[4,1024]{1,0:T(4,128)S(1)} custom-call(bf16[512,32]{1,0:T(8,128)(2,1)S(1)} %copy.6.src_hbm, bf16[512,128]{1,0:T(8,128)(2,1)S(1)} %copy-done.1, bf16[1024,1024]{1,0:T(8,128)(2,1)S(1)} %copy-done, s32[1,512]{1,0:T(1,128)S(1)} %bitcast.2, s32[1,512]{1,0:T(1,128)S(1)} %bitcast.3), custom_call_target="tpu_custom_call" | custom-call | tf_op jit(solution)/shard_map/procrustes/pallas_call | solution.py:304
  98.5 0.6 copy.8
Async XLA Ops:
  0.9 1.6 %copy-start = (bf16[1024,1024]{1,0:T(8,128)(2,1)S(1)}, bf16[1024,1024]{1,0:T(8,128)(2,1)}, u32[]{:S(2)}) copy-start(bf16[1024,1024]{1,0:T(8,128)(2,1)} %rot_hbm.1) | copy-start | bytes 6291460
  2.5 0.9 copy-start.1
  3.4 0.7 copy-start.2
  4.1 0.7 copy-start.3

commit v2 on v1

v2 whole, which is shorter than its diff:
```python
import math

import jax
import jax.numpy as jnp
from jax import lax
from jax.experimental import pallas as pl
from jax.experimental.pallas import tpu as pltpu
from jax.sharding import PartitionSpec as P

MESH = pl.DeviceIdType.MESH
F32 = jnp.float32
BF16 = jnp.bfloat16
D = 1024
W = 512
ITERS = 3
X, Y, Z = 4, 4, 8
ROWS, COLS = 2 * X, Y * Z


def hops(step, size):
    return min(step, size - step)


COL_ORDER = sorted(
    ((dy, dz) for dy in range(Y) for dz in range(Z) if dy or dz),
    key=lambda d: -hops(d[0], Y) - hops(d[1], Z))
PLANE_ORDER = sorted(
    ((dx, dk, dy) for dx in range(X) for dk in range(2) for dy in range(Y) if dx or dk or dy),
    key=lambda d: -2 * hops(d[0], X) - 3 * d[1] - 2 * hops(d[2], Y))
ROW_ORDER = [d[:2] for d in PLANE_ORDER if d[2] == 0]
Z_ORDER = (4, 3, 5, 2, 6, 1, 7)
XY_ORDER = (2, 1, 3)
NN = (((1,), (0,)), ((), ()))
NT = (((1,), (1,)), ((), ()))


def dot(a, b, dims):
    return lax.dot_general(a, b, dims, preferred_element_type=F32)


def send(src, dst, send_sem, recv_sem, device):
    pltpu.make_async_remote_copy(
        src_ref=src, dst_ref=dst, send_sem=send_sem, recv_sem=recv_sem,
        device_id=device, device_id_type=MESH,
    ).start()


def wait(ref, sem):
    pltpu.make_async_copy(ref, ref, sem).wait()


def block(i, size):
    return pl.ds(pl.multiple_of(i * size, size), size)


def body(src_hbm, tgt_hbm, rot_hbm, src_ids, tgt_ids, out_ref,
         src_t, tgt, rot, u, kt, ids, colbuf, rowbuf,
         a_mate, a_x, a_out, yb, y_out, zb, z_out, xr, own4, req, rows, c_out, c_in,
         local, zs, xs, ss, rs):
    sent = []

    def finish():
        for ref, sem in sent:
            wait(ref, sem)

    r, c = lax.axis_index("row"), lax.axis_index("col")
    x, core = r // 2, r % 2
    y, z = c // Z, c % Z
    mate = (2 * x + (1 - core), c)

    def xpeer(k):
        return (2 * ((x + k) % X) + core, c)

    def ypeer(k):
        return (r, Z * ((y + k) % Y) + z)

    def zpeer(k):
        return (r, Z * y + (z + k) % Z)

    def colpeer(d):
        return (r, Z * ((y + d[0]) % Y) + (z + d[1]) % Z)

    def rowpeer(d):
        return (2 * ((x + d[0]) % X) + (core + d[1]) % 2, c)

    def planepeer(d):
        return (rowpeer(d)[0], Z * ((y + d[2]) % Y) + z)

    mine = src_t.at[block(c, 32), :]
    load_src = pltpu.make_async_copy(src_hbm, mine, local.at[0])
    load_src.start()
    my_tgt = tgt.at[:, block(r, 128)]
    load_tgt = pltpu.make_async_copy(tgt_hbm, my_tgt, local.at[1])
    load_tgt.start()
    load_rot = pltpu.make_async_copy(rot_hbm, rot, local.at[2])
    load_rot.start()
    load_ids = [pltpu.make_async_copy(ref, ids.at[i], local.at[3 + i]) for i, ref in enumerate((src_ids, tgt_ids))]
    for load in load_ids:
        load.start()
    bar = pltpu.get_barrier_semaphore()

    near = [zpeer(k) for k in Z_ORDER] + [xpeer(k) for k in XY_ORDER] + [ypeer(k) for k in XY_ORDER] + [mate]
    for device in near:
        pl.semaphore_signal(bar, inc=1, device_id=device, device_id_type=MESH)
    load_src.wait()
    load_tgt.wait()
    pl.semaphore_wait(bar, len(near))

    for k in (1, 7, 2, 6, 3, 5, 4):
        send(mine, mine, ss.at[0], zs.at[k], zpeer(k))
    for k in (1, 3, 2):
        send(my_tgt, my_tgt, ss.at[1], xs.at[k], xpeer(k))
        send(mine, mine, ss.at[2], rs.at[2], ypeer(k))
    send(my_tgt, my_tgt, ss.at[3], rs.at[3], mate)
    sent.append((src_t.at[pl.ds(0, 224), :], ss.at[0]))
    sent.append((tgt.at[:, pl.ds(0, 384)], ss.at[1]))
    sent.append((src_t.at[pl.ds(0, 768), :], ss.at[2]))
    sent.append((tgt.at[:, pl.ds(0, 512)], ss.at[3]))

    def forward_src(k):
        got = src_t.at[block(Z * y + (z + Z - k) % Z, 32), :]
        wait(got, zs.at[k])
        for j in (1, 3, 2):
            send(got, got, ss.at[2], rs.at[2], ypeer(j))

    def forward_tgt(k):
        got = tgt.at[:, block(2 * ((x + X - k) % X) + core, 128)]
        wait(got, xs.at[k])
        send(got, got, ss.at[3], rs.at[3], mate)

    forward_src(1)
    forward_src(7)
    forward_tgt(1)
    forward_tgt(3)
    forward_src(2)
    forward_src(6)
    forward_tgt(2)
    forward_src(3)
    forward_src(5)
    forward_src(4)

    wait(tgt.at[:, pl.ds(0, 512)], rs.at[3])
    load_rot.wait()
    tv = tgt[...].astype(F32)
    tsum = jnp.sum(tv * tv, axis=1, keepdims=True)
    tscale = lax.rsqrt(tsum * (1.0 / D) + 1e-06) * (1.0 / math.sqrt(D))
    u[...] = (dot(tgt[...], rot[...], NT) * tscale).astype(BF16)
    tscale_l = jnp.transpose(jnp.broadcast_to(tscale, (W, 128)))[0:1, :]
    for load in load_ids:
        load.wait()
    src_mass = lax.rsqrt(1000.0 + ids[0].astype(F32))
    tgt_mass = lax.rsqrt(1000.0 + ids[1].astype(F32))

    wait(src_t.at[pl.ds(0, 24 * 32), :], rs.at[2])
    sv = src_t[...].astype(F32)
    ssum = jnp.sum(sv * sv, axis=0, keepdims=True)
    sscale = lax.rsqrt(ssum * (1.0 / D) + 1e-06) * (1.0 / math.sqrt(D))
    kt[...] = jnp.exp(dot(u[...], src_t[...], NN) * (sscale * (1.0 / 0.03))).astype(BF16)

    row8 = lax.broadcasted_iota(jnp.int32, (8, W), 0)

    def matvec(v, dims):
        high = v.astype(BF16).astype(F32)
        both = jnp.where(row8 == 0, high, jnp.where(row8 == 1, v - high, 0.0)).astype(BF16)
        return jnp.sum(dot(both, kt[...], dims), axis=0, keepdims=True)

    def sum_col(part, it):
        colbuf[it, c] = part

        for d in COL_ORDER:
            send(colbuf.at[it, c], colbuf.at[it, c], ss.at[4 + it], rs.at[4 + it], colpeer(d))
        sent.append((colbuf.at[it, pl.ds(0, COLS - 1)], ss.at[4 + it]))
        wait(colbuf.at[it, pl.ds(0, COLS - 1)], rs.at[4 + it])
        return jnp.sum(colbuf[it], axis=0)

    def start_row(part, it):
        rowbuf[it, r] = part
        for d in ROW_ORDER:
            send(rowbuf.at[it, r], rowbuf.at[it, r], ss.at[7 + it], rs.at[7 + it], rowpeer(d))
        sent.append((rowbuf.at[it, pl.ds(0, ROWS - 1)], ss.at[7 + it]))

    def end_row(it):
        wait(rowbuf.at[it, pl.ds(0, ROWS - 1)], rs.at[7 + it])
        return jnp.sum(rowbuf[it], axis=0)

    tgt_scale = jnp.ones((1, W), F32)
    for it in range(ITERS):
        src_scale = src_mass / sum_col(matvec(tgt_scale, NN), it)
        start_row(matvec(src_scale, NT), it)
        if it < ITERS - 1:
            tgt_scale = tgt_mass / end_row(it)

    kt[...] = (kt[...].astype(F32) * (src_scale * sscale)).astype(BF16)
    for k in (2, 1, 3, 0):
        a_out[k] = dot(src_t[block(2 * ((x + k) % X) + (1 - core), 128), :], kt[...], NT).astype(BF16)
        send(a_out.at[k], a_mate.at[k], ss.at[10], xs.at[4 + k], mate)
    sent.append((a_mate, ss.at[10]))
    for k in (2, 1, 3, 0):
        half = dot(src_t[block(2 * ((x + k) % X) + core, 128), :], kt[...], NT)
        wait(a_mate.at[k], xs.at[4 + k])
        half = half + a_mate[k].astype(F32)
        if k:
            a_out[X + k] = half.astype(BF16)
            send(a_out.at[X + k], a_x.at[k - 1], ss.at[11], rs.at[11], xpeer(k))
    sent.append((a_x, ss.at[11]))
    tgt_scale = tgt_mass / end_row(ITERS - 1)
    wait(a_x, rs.at[11])
    total = half + ((a_x[0].astype(F32) + a_x[1].astype(F32)) + a_x[2].astype(F32))
    total = (total * (tgt_scale * tscale_l)).astype(BF16)
    to = lax.broadcasted_iota(jnp.int32, (128, 128), 0)
    to = 32 * (to // 4 % 4) + 4 * (to // 16) + to % 4
    order = (lax.broadcasted_iota(jnp.int32, (128, 128), 1) == to).astype(BF16)
    total = dot(order, total, NN).astype(BF16)

    def rows16(i):
        return pl.ds(pl.multiple_of(16 * i, 16), 16)

    cross = dot(total, tgt[...], NN)
    for j in range(Y):
        y_out[j] = cross[:, 256 * j:256 * (j + 1)].astype(BF16)
    for k in Z_ORDER + (0,):
        chunk = rows16((z + k) % Z)
        for j in XY_ORDER:
            send(y_out.at[(y + j) % Y, chunk], yb.at[j - 1, chunk], ss.at[12], zs.at[8 + k], ypeer(j))
    sent.append((yb, ss.at[12]))
    for k in Z_ORDER + (0,):
        chunk = rows16((z + k) % Z)
        wait(yb.at[:, chunk], zs.at[8 + k])
        part = (y_out[y, chunk].astype(F32) + yb[0, chunk].astype(F32)) + (
            yb[1, chunk].astype(F32) + yb[2, chunk].astype(F32))
        if k:
            z_out[k - 1] = part.astype(BF16)
            send(z_out.at[k - 1], zb.at[k - 1], ss.at[13], rs.at[13], zpeer(k))
    sent.append((zb, ss.at[13]))
    wait(zb, rs.at[13])
    own = part + jnp.sum(zb[...].astype(F32), axis=0)

    def cell(i, j):
        return xr.at[rows16(i), block(j, 256)]

    xr[rows16(z), block(y, 256)] = own.astype(BF16)
    for k in Z_ORDER:
        send(cell(z, y), cell(z, y), ss.at[14], zs.at[16 + k], zpeer(k))
    sent.append((xr.at[pl.ds(0, 112), pl.ds(0, 256)], ss.at[14]))
    for j in range(Y):
        own4[j] = own[4 * j:4 * (j + 1)]
    for d in PLANE_ORDER:
        send(own4.at[(y + d[2]) % Y], req.at[Y * r + y], ss.at[15], rs.at[15], planepeer(d))
    sent.append((req.at[pl.ds(0, ROWS * Y - 1)], ss.at[15]))
    req[Y * r + y] = own4[y]
    for j in XY_ORDER:
        send(cell(z, y), cell(z, y), ss.at[16], rs.at[16], ypeer(j))
    for k in (1, 7, 2, 6, 3, 5, 4):
        got = cell((z + Z - k) % Z, y)
        wait(got, zs.at[16 + k])
        for j in XY_ORDER:
            send(got, got, ss.at[16], rs.at[16], ypeer(j))
    sent.append((xr.at[pl.ds(0, 96), :], ss.at[16]))
    wait(req.at[pl.ds(0, ROWS * Y - 1)], rs.at[15])
    for i in range(ROWS):
        for j in range(Y):
            rows[4 * i:4 * (i + 1), 256 * j:256 * (j + 1)] = req[Y * i + j]
    wait(xr.at[pl.ds(0, 96), :], rs.at[16])

    xv = xr[...].astype(F32)
    square = jnp.sum(jnp.sum(xv * xv, axis=0, keepdims=True), axis=1, keepdims=True)
    gram = dot(rows[...].astype(BF16), xr[...], NT) * (1.0 / (square * (1.0 / (128 * D)) + 1e-30))
    cubic = dot(gram.astype(BF16), xr[...], NN)
    for i in range(ROWS):
        c_out[i, :, 0:D] = cubic[4 * i:4 * (i + 1)]
        c_out[i, :, D:] = jnp.broadcast_to(square, (4, 128))
    for d in ROW_ORDER:
        peer = rowpeer(d)
        send(c_out.at[peer[0]], c_in.at[r], ss.at[17], rs.at[17], peer)
    sent.append((c_in.at[pl.ds(0, ROWS - 1)], ss.at[17]))
    c_in[r] = c_out[r]
    linear = jnp.concatenate([req[Y * r + j] for j in range(Y)], axis=1)
    wait(c_in.at[pl.ds(0, ROWS - 1)], rs.at[17])
    squares = [c_in[i, 0:1, D:D + 1] for i in range(ROWS)]
    mean = sum(squares) * (1.0 / (D * D)) + 1e-30
    inverse = 1.0 / (mean * (4.0 * D))
    cubic = sum(
        c_in[i, :, 0:D] * ((squares[i] * (1.0 / (128 * D)) + 1e-30) * inverse) for i in range(ROWS))
    scale = lax.rsqrt(mean) * (1.0 / (2.0 * math.sqrt(D)))
    out_ref[...] = (math.sqrt(D) * scale) * (1.5 * linear - 0.5 * cubic)
    finish()


def shards(src_emb, tgt_emb, rotation, src_ids, tgt_ids):
    vmem = pltpu.VMEM
    scratch = [
        vmem((D, W), BF16),
        vmem((W, D), BF16),
        vmem((D, D), BF16),
        vmem((W, D), BF16),
        vmem((W, W), BF16),
        vmem((2, 1, W), jnp.int32),
        vmem((ITERS, COLS, 1, W), F32),
        vmem((ITERS, ROWS, 1, W), F32),
        vmem((X, 128, W), BF16),
        vmem((X - 1, 128, W), BF16),
        vmem((2 * X, 128, W), BF16),
        vmem((Y - 1, 128, 256), BF16),
        vmem((Y, 128, 256), BF16),
        vmem((Z - 1, 16, 256), BF16),
        vmem((Z - 1, 16, 256), BF16),
        vmem((128, D), BF16),
        vmem((Y, 4, 256), F32),
        vmem((ROWS * Y, 4, 256), F32),
        vmem((32, D), F32),
        vmem((ROWS, 4, D + 128), F32),
        vmem((ROWS, 4, D + 128), F32),
        pltpu.SemaphoreType.DMA((5,)),
        pltpu.SemaphoreType.DMA((24,)),
        pltpu.SemaphoreType.DMA((8,)),
        pltpu.SemaphoreType.DMA((18,)),
        pltpu.SemaphoreType.DMA((18,)),
    ]
    hbm = pl.BlockSpec(memory_space=pltpu.HBM)
    here = pl.BlockSpec(memory_space=pltpu.VMEM)
    return pl.pallas_call(
        body,
        out_shape=jax.ShapeDtypeStruct((4, D), F32),
        in_specs=[hbm] * 5,
        out_specs=here,
        scratch_shapes=scratch,
        compiler_params=pltpu.CompilerParams(
            collective_id=0, has_side_effects=True, vmem_limit_bytes=63 * 2**20
        ),
        name="procrustes",
    )(src_emb.T, tgt_emb, rotation, src_ids.reshape(1, W), tgt_ids.reshape(1, W))


def solution(mesh):
    return jax.shard_map(
        shards,
        mesh=mesh,
        in_specs=(P("row", "col"), P("col", "row"), P(), P("row"), P("col")),
        out_specs=P(("row", "col"), None),
        check_vma=False,
    )
```

time: 99.3 us -> 85.2 us (0.86)
  Pallas kernels: 93.7 us -> 83.7 us
  local copies, waits for them, and re-layouts: 5.34 us -> 1.32 us
    pallas_call x1, Pallas kernels: 93.7 us -> 83.7 us  [shards(): pl.pallas_call(body, out_shape=jax.ShapeDtypeStruct((4, D), F32), in_spec...]
    unnamed x10 -> x1, local copies, waits for them, and re-layouts: 5.34 us -> 1.32 us
where the time goes in v2:
time: 85.2 us; the launch traced here: 85 us
  Pallas kernels  83.7 us (98%)
  local copies, waits for them, and re-layouts  1.32 us (2%)
    pallas_call x1, Pallas kernels, shards(): pl.pallas_call(body, out_shape=jax.ShapeDtypeStruct((4, D), F32), in_spec...  83.7 us

profile of v2, /device:TPU:1, one launch (start us, length us, event | category | flops | bytes accessed | tf_op | source)
XLA Modules:
  0.0 85.0 jit_solution(17264801796098066912)
XLA Ops:
  0.0 83.7 %procrustes.1 = f32[4,1024]{1,0:T(4,128)} custom-call(bf16[32,512]{1,0:T(8,128)(2,1)} %bitcast.3, bf16[512,128]{1,0:T(8,128)(2,1)} %tgt_hbm.1, bf16[1024,1024]{1,0:T(8,128)(2,1)} %rot_hbm.1, s32[1,512]{1,0:T(1,128)} %bitcast.4, s32[1,512]{1,0:T(1,128)} %bitcast.5), custom_call_target="tpu_custom_call" | custom-call | tf_op jit(solution)/shard_map/procrustes/pallas_call | solution.py:321
  83.7 1.3 %copy.7 = f32[4,1024]{1,0:T(4,128)} copy(f32[4,1024]{1,0:T(4,128)} %procrustes.1) | data formatting | bytes 32768

commit v3 on v2

--- a/solution.py
+++ b/solution.py
@@ -29,6 +29,8 @@
     key=lambda d: -2 * hops(d[0], X) - 3 * d[1] - 2 * hops(d[2], Y))
 ROW_ORDER = [d[:2] for d in PLANE_ORDER if d[2] == 0]
 Z_ORDER = (4, 3, 5, 2, 6, 1, 7)
+Z_NEAR = (0, 1, 7, 2, 6, 3, 5, 4)
+UP, DOWN = (0, 7, 6), (1, 2)
 XY_ORDER = (2, 1, 3)
 NN = (((1,), (0,)), ((), ()))
 NT = (((1,), (1,)), ((), ()))
@@ -54,8 +56,8 @@
 
 
 def body(src_hbm, tgt_hbm, rot_hbm, src_ids, tgt_ids, out_ref,
-         src_t, tgt, rot, u, kt, ids, colbuf, rowbuf,
-         a_mate, a_x, a_out, yb, y_out, zb, z_out, xr, own4, req, rows, c_out, c_in,
+         src_t, ordered, tgt, rot, u, kt, ids, colbuf, rowbuf,
+         a_mate, a_x, a_out, yb, y_out, y_mine, zb, z_out, xr, own4, req, rows, c_out, c_in,
          local, zs, xs, ss, rs):
     sent = []
 
@@ -86,14 +88,19 @@
     def planepeer(d):
         return (rowpeer(d)[0], Z * ((y + d[2]) % Y) + z)
 
-    mine = src_t.at[block(c, 32), :]
+    def feature(i, j):
+        return pl.ds(pl.multiple_of(128 * i + 32 * j, 32), 32)
+
+    mine = src_t.at[feature(z, y)]
     load_src = pltpu.make_async_copy(src_hbm, mine, local.at[0])
     load_src.start()
     my_tgt = tgt.at[:, block(r, 128)]
     load_tgt = pltpu.make_async_copy(tgt_hbm, my_tgt, local.at[1])
     load_tgt.start()
-    load_rot = pltpu.make_async_copy(rot_hbm, rot, local.at[2])
-    load_rot.start()
+    for i in range(Z):
+        for j in range(Y):
+            pltpu.make_async_copy(
+                rot_hbm.at[pl.ds(32 * (Z * j + i), 32)], rot.at[pl.ds(128 * i + 32 * j, 32)], local.at[2]).start()
     load_ids = [pltpu.make_async_copy(ref, ids.at[i], local.at[3 + i]) for i, ref in enumerate((src_ids, tgt_ids))]
     for load in load_ids:
         load.start()
@@ -106,23 +113,38 @@
     load_tgt.wait()
     pl.semaphore_wait(bar, len(near))
 
-    for k in (1, 7, 2, 6, 3, 5, 4):
+    def over_y(k):
+        got = src_t.at[feature((z + Z - k) % Z, y)]
+        passed = zs.at[24 + k]
+        rest = zs.at[32 + k]
+        send(got, got, ss.at[2], passed if k in UP else rest, ypeer(1))
+        send(got, got, ss.at[2], passed if k in DOWN else rest, ypeer(3))
+        if k not in UP + DOWN:
+            send(got, got, ss.at[2], rest, ypeer(2))
+
+    def forward_src(k):
+        wait(mine, zs.at[k])
+        over_y(k)
+
+    def pass_on(k):
+        step = 1 if k in UP else 3
+        got = src_t.at[feature((z + Z - k) % Z, (y + Y - step) % Y)]
+        wait(got, zs.at[24 + k])
+        send(got, got, ss.at[2], zs.at[32 + k], ypeer(step))
+
+    for k in (1, 7):
         send(mine, mine, ss.at[0], zs.at[k], zpeer(k))
+    over_y(0)
     for k in (1, 3, 2):
         send(my_tgt, my_tgt, ss.at[1], xs.at[k], xpeer(k))
-        send(mine, mine, ss.at[2], rs.at[2], ypeer(k))
+    for k in (2, 6, 3, 5, 4):
+        send(mine, mine, ss.at[0], zs.at[k], zpeer(k))
     send(my_tgt, my_tgt, ss.at[3], rs.at[3], mate)
     sent.append((src_t.at[pl.ds(0, 224), :], ss.at[0]))
     sent.append((tgt.at[:, pl.ds(0, 384)], ss.at[1]))
     sent.append((src_t.at[pl.ds(0, 768), :], ss.at[2]))
     sent.append((tgt.at[:, pl.ds(0, 512)], ss.at[3]))
 
-    def forward_src(k):
-        got = src_t.at[block(Z * y + (z + Z - k) % Z, 32), :]
-        wait(got, zs.at[k])
-        for j in (1, 3, 2):
-            send(got, got, ss.at[2], rs.at[2], ypeer(j))
-
     def forward_tgt(k):
         got = tgt.at[:, block(2 * ((x + X - k) % X) + core, 128)]
         wait(got, xs.at[k])
@@ -130,32 +152,40 @@
 
     forward_src(1)
     forward_src(7)
+    pass_on(0)
     forward_tgt(1)
     forward_tgt(3)
     forward_src(2)
     forward_src(6)
+    pass_on(1)
+    pass_on(7)
     forward_tgt(2)
     forward_src(3)
     forward_src(5)
+    pass_on(2)
+    pass_on(6)
     forward_src(4)
 
     wait(tgt.at[:, pl.ds(0, 512)], rs.at[3])
-    load_rot.wait()
+    wait(rot, local.at[2])
     tv = tgt[...].astype(F32)
     tsum = jnp.sum(tv * tv, axis=1, keepdims=True)
     tscale = lax.rsqrt(tsum * (1.0 / D) + 1e-06) * (1.0 / math.sqrt(D))
     u[...] = (dot(tgt[...], rot[...], NT) * tscale).astype(BF16)
-    tscale_l = jnp.transpose(jnp.broadcast_to(tscale, (W, 128)))[0:1, :]
     for load in load_ids:
         load.wait()
-    src_mass = lax.rsqrt(1000.0 + ids[0].astype(F32))
-    tgt_mass = lax.rsqrt(1000.0 + ids[1].astype(F32))
-
-    wait(src_t.at[pl.ds(0, 24 * 32), :], rs.at[2])
-    sv = src_t[...].astype(F32)
-    ssum = jnp.sum(sv * sv, axis=0, keepdims=True)
-    sscale = lax.rsqrt(ssum * (1.0 / D) + 1e-06) * (1.0 / math.sqrt(D))
-    kt[...] = jnp.exp(dot(u[...], src_t[...], NN) * (sscale * (1.0 / 0.03))).astype(BF16)
+    logits = jnp.zeros((W, W), F32)
+    square = jnp.zeros((1, W), F32)
+    for k in Z_NEAR:
+        i = (z + Z - k) % Z
+        here = src_t.at[block(i, 128)]
+        wait(src_t.at[pl.ds(0, 64 if k in UP + DOWN else 96)], zs.at[32 + k])
+        part = here[...]
+        logits = logits + dot(u[:, block(i, 128)], part, NN)
+        part = part.astype(F32)
+        square = square + jnp.sum(part * part, axis=0, keepdims=True)
+    sscale = lax.rsqrt(square * (1.0 / D) + 1e-06) * (1.0 / math.sqrt(D))
+    kt[...] = jnp.exp(logits * (sscale * (1.0 / 0.03))).astype(BF16)
 
     row8 = lax.broadcasted_iota(jnp.int32, (8, W), 0)
 
@@ -164,12 +194,23 @@
         both = jnp.where(row8 == 0, high, jnp.where(row8 == 1, v - high, 0.0)).astype(BF16)
         return jnp.sum(dot(both, kt[...], dims), axis=0, keepdims=True)
 
+    def meanwhile():
+        to = lax.broadcasted_iota(jnp.int32, (128, 128), 0)
+        to = 32 * (to // 4 % 4) + 4 * (to // 16) + to % 4
+        order = (lax.broadcasted_iota(jnp.int32, (128, 128), 1) == to).astype(BF16)
+        for i in range(ROWS):
+            natural = [src_t[128 * j + 32 * (i // 2):128 * j + 32 * (i // 2) + 32]
+                       for j in range(4 * (i % 2), 4 * (i % 2) + 4)]
+            ordered[i] = dot(order, jnp.concatenate(natural, axis=0), NN).astype(BF16)
+
     def sum_col(part, it):
         colbuf[it, c] = part
 
         for d in COL_ORDER:
             send(colbuf.at[it, c], colbuf.at[it, c], ss.at[4 + it], rs.at[4 + it], colpeer(d))
         sent.append((colbuf.at[it, pl.ds(0, COLS - 1)], ss.at[4 + it]))
+        if it == 0:
+            meanwhile()
         wait(colbuf.at[it, pl.ds(0, COLS - 1)], rs.at[4 + it])
         return jnp.sum(colbuf[it], axis=0)
 
@@ -183,50 +224,49 @@
         wait(rowbuf.at[it, pl.ds(0, ROWS - 1)], rs.at[7 + it])
         return jnp.sum(rowbuf[it], axis=0)
 
+    src_mass = lax.rsqrt(1000.0 + ids[0].astype(F32))
+    tgt_mass = lax.rsqrt(1000.0 + ids[1].astype(F32))
     tgt_scale = jnp.ones((1, W), F32)
     for it in range(ITERS):
         src_scale = src_mass / sum_col(matvec(tgt_scale, NN), it)
-        start_row(matvec(src_scale, NT), it)
         if it < ITERS - 1:
+            start_row(matvec(src_scale, NT), it)
             tgt_scale = tgt_mass / end_row(it)
 
-    kt[...] = (kt[...].astype(F32) * (src_scale * sscale)).astype(BF16)
+    plan = (kt[...].astype(F32) * (src_scale * sscale)).astype(BF16)
     for k in (2, 1, 3, 0):
-        a_out[k] = dot(src_t[block(2 * ((x + k) % X) + (1 - core), 128), :], kt[...], NT).astype(BF16)
+        a_out[k] = dot(ordered[2 * ((x + k) % X) + (1 - core)], plan, NT).astype(BF16)
         send(a_out.at[k], a_mate.at[k], ss.at[10], xs.at[4 + k], mate)
     sent.append((a_mate, ss.at[10]))
     for k in (2, 1, 3, 0):
-        half = dot(src_t[block(2 * ((x + k) % X) + core, 128), :], kt[...], NT)
+        half = dot(ordered[2 * ((x + k) % X) + core], plan, NT)
         wait(a_mate.at[k], xs.at[4 + k])
         half = half + a_mate[k].astype(F32)
         if k:
             a_out[X + k] = half.astype(BF16)
             send(a_out.at[X + k], a_x.at[k - 1], ss.at[11], rs.at[11], xpeer(k))
     sent.append((a_x, ss.at[11]))
+    start_row(matvec(src_scale, NT), ITERS - 1)
+    tscale_l = jnp.transpose(jnp.broadcast_to(tscale, (W, 128)))[0:1, :]
     tgt_scale = tgt_mass / end_row(ITERS - 1)
     wait(a_x, rs.at[11])
     total = half + ((a_x[0].astype(F32) + a_x[1].astype(F32)) + a_x[2].astype(F32))
     total = (total * (tgt_scale * tscale_l)).astype(BF16)
-    to = lax.broadcasted_iota(jnp.int32, (128, 128), 0)
-    to = 32 * (to // 4 % 4) + 4 * (to // 16) + to % 4
-    order = (lax.broadcasted_iota(jnp.int32, (128, 128), 1) == to).astype(BF16)
-    total = dot(order, total, NN).astype(BF16)
 
     def rows16(i):
         return pl.ds(pl.multiple_of(16 * i, 16), 16)
 
-    cross = dot(total, tgt[...], NN)
-    for j in range(Y):
-        y_out[j] = cross[:, 256 * j:256 * (j + 1)].astype(BF16)
-    for k in Z_ORDER + (0,):
-        chunk = rows16((z + k) % Z)
-        for j in XY_ORDER:
-            send(y_out.at[(y + j) % Y, chunk], yb.at[j - 1, chunk], ss.at[12], zs.at[8 + k], ypeer(j))
+    for j in XY_ORDER:
+        y_out[j - 1] = dot(total, tgt[:, block((y + j) % Y, 256)], NN).astype(BF16)
+        for k in Z_ORDER + (0,):
+            chunk = rows16((z + k) % Z)
+            send(y_out.at[j - 1, chunk], yb.at[j - 1, chunk], ss.at[12], zs.at[8 + k], ypeer(j))
+    y_mine[...] = dot(total, tgt[:, block(y, 256)], NN)
     sent.append((yb, ss.at[12]))
     for k in Z_ORDER + (0,):
         chunk = rows16((z + k) % Z)
         wait(yb.at[:, chunk], zs.at[8 + k])
-        part = (y_out[y, chunk].astype(F32) + yb[0, chunk].astype(F32)) + (
+        part = (y_mine[chunk] + yb[0, chunk].astype(F32)) + (
             yb[1, chunk].astype(F32) + yb[2, chunk].astype(F32))
         if k:
             z_out[k - 1] = part.astype(BF16)
@@ -290,6 +330,7 @@
     vmem = pltpu.VMEM
     scratch = [
         vmem((D, W), BF16),
+        vmem((ROWS, 128, W), BF16),
         vmem((W, D), BF16),
         vmem((D, D), BF16),
         vmem((W, D), BF16),
@@ -301,7 +342,8 @@
         vmem((X - 1, 128, W), BF16),
         vmem((2 * X, 128, W), BF16),
         vmem((Y - 1, 128, 256), BF16),
-        vmem((Y, 128, 256), BF16),
+        vmem((Y - 1, 128, 256), BF16),
+        vmem((128, 256), F32),
         vmem((Z - 1, 16, 256), BF16),
         vmem((Z - 1, 16, 256), BF16),
         vmem((128, D), BF16),
@@ -311,7 +353,7 @@
         vmem((ROWS, 4, D + 128), F32),
         vmem((ROWS, 4, D + 128), F32),
         pltpu.SemaphoreType.DMA((5,)),
-        pltpu.SemaphoreType.DMA((24,)),
+        pltpu.SemaphoreType.DMA((40,)),
         pltpu.SemaphoreType.DMA((8,)),
         pltpu.SemaphoreType.DMA((18,)),
         pltpu.SemaphoreType.DMA((18,)),

time: 85.2 us -> 86.4 us (1.014)
  Pallas kernels: 83.7 us -> 84.9 us
    pallas_call x1, Pallas kernels: 83.7 us -> 84.9 us  [shards(): pl.pallas_call(body, out_shape=jax.ShapeDtypeStruct((4, D), F32), in_spec...]
where the time goes in v3:
time: 86.4 us; the launch traced here: 86.2 us
  Pallas kernels  84.9 us (98%)
  local copies, waits for them, and re-layouts  1.32 us (2%)
    pallas_call x1, Pallas kernels, shards(): pl.pallas_call(body, out_shape=jax.ShapeDtypeStruct((4, D), F32), in_spec...  84.9 us

profile of v3, /device:TPU:1, one launch (start us, length us, event | category | flops | bytes accessed | tf_op | source)
XLA Modules:
  0.0 86.2 jit_solution(17053970080154056242)
XLA Ops:
  0.0 84.9 %procrustes.1 = f32[4,1024]{1,0:T(4,128)} custom-call(bf16[32,512]{1,0:T(8,128)(2,1)} %bitcast.3, bf16[512,128]{1,0:T(8,128)(2,1)} %tgt_hbm.1, bf16[1024,1024]{1,0:T(8,128)(2,1)} %rot_hbm.1, s32[1,512]{1,0:T(1,128)} %bitcast.4, s32[1,512]{1,0:T(1,128)} %bitcast.5), custom_call_target="tpu_custom_call" | custom-call | tf_op jit(solution)/shard_map/procrustes/pallas_call | solution.py:363
  84.9 1.3 %copy.7 = f32[4,1024]{1,0:T(4,128)} copy(f32[4,1024]{1,0:T(4,128)} %procrustes.1) | data formatting | bytes 32768

commit v4 on v3

--- a/solution.py
+++ b/solution.py
@@ -30,7 +30,9 @@
 ROW_ORDER = [d[:2] for d in PLANE_ORDER if d[2] == 0]
 Z_ORDER = (4, 3, 5, 2, 6, 1, 7)
 Z_NEAR = (0, 1, 7, 2, 6, 3, 5, 4)
-UP, DOWN = (0, 7, 6), (1, 2)
+PARTS = 2
+ROWS_IN = 128 // PARTS
+CHUNKS = Z // PARTS
 XY_ORDER = (2, 1, 3)
 NN = (((1,), (0,)), ((), ()))
 NT = (((1,), (1,)), ((), ()))
@@ -57,7 +59,7 @@
 
 def body(src_hbm, tgt_hbm, rot_hbm, src_ids, tgt_ids, out_ref,
          src_t, ordered, tgt, rot, u, kt, ids, colbuf, rowbuf,
-         a_mate, a_x, a_out, yb, y_out, y_mine, zb, z_out, xr, own4, req, rows, c_out, c_in,
+         a_mate, a_out, a_x, x_out, yb, y_out, y_mine, zb, z_out, xr, own4, req, rows, c_out, c_in,
          local, zs, xs, ss, rs):
     sent = []
 
@@ -115,34 +117,26 @@
 
     def over_y(k):
         got = src_t.at[feature((z + Z - k) % Z, y)]
-        passed = zs.at[24 + k]
-        rest = zs.at[32 + k]
-        send(got, got, ss.at[2], passed if k in UP else rest, ypeer(1))
-        send(got, got, ss.at[2], passed if k in DOWN else rest, ypeer(3))
-        if k not in UP + DOWN:
-            send(got, got, ss.at[2], rest, ypeer(2))
-
-    def forward_src(k):
         wait(mine, zs.at[k])
-        over_y(k)
-
-    def pass_on(k):
-        step = 1 if k in UP else 3
-        got = src_t.at[feature((z + Z - k) % Z, (y + Y - step) % Y)]
-        wait(got, zs.at[24 + k])
-        send(got, got, ss.at[2], zs.at[32 + k], ypeer(step))
-
-    for k in (1, 7):
+        for j in (1, 3, 2):
+            send(got, got, ss.at[2], zs.at[32 + k], ypeer(j))
+
+    def over_z(j):
+        got = src_t.at[feature(z, (y + Y - j) % Y)]
+        wait(got, zs.at[24 + j])
+        for k in (1, 7):
+            send(got, got, ss.at[0], zs.at[32 + k], zpeer(k))
+
+    for j in (1, 3, 2):
+        send(mine, mine, ss.at[2], zs.at[24 + j], ypeer(j))
+    for k in (2, 6, 3, 5, 4, 1, 7):
         send(mine, mine, ss.at[0], zs.at[k], zpeer(k))
-    over_y(0)
     for k in (1, 3, 2):
         send(my_tgt, my_tgt, ss.at[1], xs.at[k], xpeer(k))
-    for k in (2, 6, 3, 5, 4):
-        send(mine, mine, ss.at[0], zs.at[k], zpeer(k))
     send(my_tgt, my_tgt, ss.at[3], rs.at[3], mate)
-    sent.append((src_t.at[pl.ds(0, 224), :], ss.at[0]))
+    sent.append((src_t.at[pl.ds(0, 13 * 32), :], ss.at[0]))
     sent.append((tgt.at[:, pl.ds(0, 384)], ss.at[1]))
-    sent.append((src_t.at[pl.ds(0, 768), :], ss.at[2]))
+    sent.append((src_t.at[pl.ds(0, 18 * 32), :], ss.at[2]))
     sent.append((tgt.at[:, pl.ds(0, 512)], ss.at[3]))
 
     def forward_tgt(k):
@@ -150,21 +144,17 @@
         wait(got, xs.at[k])
         send(got, got, ss.at[3], rs.at[3], mate)
 
-    forward_src(1)
-    forward_src(7)
-    pass_on(0)
+    over_z(1)
+    over_z(3)
+    over_y(2)
+    over_y(6)
+    over_z(2)
     forward_tgt(1)
     forward_tgt(3)
-    forward_src(2)
-    forward_src(6)
-    pass_on(1)
-    pass_on(7)
+    over_y(3)
+    over_y(5)
     forward_tgt(2)
-    forward_src(3)
-    forward_src(5)
-    pass_on(2)
-    pass_on(6)
-    forward_src(4)
+    over_y(4)
 
     wait(tgt.at[:, pl.ds(0, 512)], rs.at[3])
     wait(rot, local.at[2])
@@ -179,7 +169,10 @@
     for k in Z_NEAR:
         i = (z + Z - k) % Z
         here = src_t.at[block(i, 128)]
-        wait(src_t.at[pl.ds(0, 64 if k in UP + DOWN else 96)], zs.at[32 + k])
+        if k in (1, 7):
+            wait(mine, zs.at[k])
+        if k:
+            wait(src_t.at[pl.ds(0, 96)], zs.at[32 + k])
         part = here[...]
         logits = logits + dot(u[:, block(i, 128)], part, NN)
         part = part.astype(F32)
@@ -195,8 +188,11 @@
         return jnp.sum(dot(both, kt[...], dims), axis=0, keepdims=True)
 
     def meanwhile():
-        to = lax.broadcasted_iota(jnp.int32, (128, 128), 0)
-        to = 32 * (to // 4 % 4) + 4 * (to // 16) + to % 4
+        at = lax.broadcasted_iota(jnp.int32, (128, 128), 0)
+        step = jnp.zeros((128, 128), jnp.int32)
+        for i, k in enumerate(Z_ORDER):
+            step = jnp.where(at // 16 == i, k, step)
+        to = 32 * (at // 4 % 4) + 4 * ((z + step) % Z) + at % 4
         order = (lax.broadcasted_iota(jnp.int32, (128, 128), 1) == to).astype(BF16)
         for i in range(ROWS):
             natural = [src_t[128 * j + 32 * (i // 2):128 * j + 32 * (i // 2) + 32]
@@ -234,51 +230,54 @@
             tgt_scale = tgt_mass / end_row(it)
 
     plan = (kt[...].astype(F32) * (src_scale * sscale)).astype(BF16)
-    for k in (2, 1, 3, 0):
-        a_out[k] = dot(ordered[2 * ((x + k) % X) + (1 - core)], plan, NT).astype(BF16)
-        send(a_out.at[k], a_mate.at[k], ss.at[10], xs.at[4 + k], mate)
+    def some_rows(k, h):
+        first = pl.ds(ROWS_IN * h, ROWS_IN)
+        return jnp.concatenate([ordered[2 * ((x + j) % X) + k, first] for j in range(X)], axis=0)
+
+    for h in range(PARTS):
+        a_out[h] = dot(some_rows(1 - core, h), plan, NT).astype(BF16)
+        send(a_out.at[h], a_mate.at[h], ss.at[10], xs.at[4 + h], mate)
     sent.append((a_mate, ss.at[10]))
-    for k in (2, 1, 3, 0):
-        half = dot(ordered[2 * ((x + k) % X) + core], plan, NT)
-        wait(a_mate.at[k], xs.at[4 + k])
-        half = half + a_mate[k].astype(F32)
-        if k:
-            a_out[X + k] = half.astype(BF16)
-            send(a_out.at[X + k], a_x.at[k - 1], ss.at[11], rs.at[11], xpeer(k))
-    sent.append((a_x, ss.at[11]))
     start_row(matvec(src_scale, NT), ITERS - 1)
     tscale_l = jnp.transpose(jnp.broadcast_to(tscale, (W, 128)))[0:1, :]
-    tgt_scale = tgt_mass / end_row(ITERS - 1)
-    wait(a_x, rs.at[11])
-    total = half + ((a_x[0].astype(F32) + a_x[1].astype(F32)) + a_x[2].astype(F32))
-    total = (total * (tgt_scale * tscale_l)).astype(BF16)
-
-    def rows16(i):
-        return pl.ds(pl.multiple_of(16 * i, 16), 16)
-
-    for j in XY_ORDER:
-        y_out[j - 1] = dot(total, tgt[:, block((y + j) % Y, 256)], NN).astype(BF16)
-        for k in Z_ORDER + (0,):
-            chunk = rows16((z + k) % Z)
-            send(y_out.at[j - 1, chunk], yb.at[j - 1, chunk], ss.at[12], zs.at[8 + k], ypeer(j))
-    y_mine[...] = dot(total, tgt[:, block(y, 256)], NN)
+    kept = []
+    for h in range(PARTS):
+        half = dot(some_rows(core, h), plan, NT)
+        wait(a_mate.at[h], xs.at[4 + h])
+        half = half + a_mate[h].astype(F32)
+        kept.append(half[0:ROWS_IN])
+        for k in (2, 1, 3):
+            x_out[h, k - 1] = half[ROWS_IN * k:ROWS_IN * (k + 1)].astype(BF16)
+            send(x_out.at[h, k - 1], a_x.at[h, k - 1], ss.at[11], xs.at[8 + h], xpeer(k))
+    sent.append((a_x, ss.at[11]))
+    factor = (tgt_mass / end_row(ITERS - 1)) * tscale_l
+
+    for h in range(PARTS):
+        wait(a_x.at[h], xs.at[8 + h])
+        total = kept[h] + ((a_x[h, 0].astype(F32) + a_x[h, 1].astype(F32)) + a_x[h, 2].astype(F32))
+        total = (total * factor).astype(BF16)
+        for j in XY_ORDER:
+            y_out[h, j - 1] = dot(total, tgt[:, block((y + j) % Y, 256)], NN).astype(BF16)
+            send(y_out.at[h, j - 1], yb.at[h, j - 1], ss.at[12], xs.at[12 + h], ypeer(j))
+        y_mine[h] = dot(total, tgt[:, block(y, 256)], NN)
     sent.append((yb, ss.at[12]))
-    for k in Z_ORDER + (0,):
-        chunk = rows16((z + k) % Z)
-        wait(yb.at[:, chunk], zs.at[8 + k])
-        part = (y_mine[chunk] + yb[0, chunk].astype(F32)) + (
-            yb[1, chunk].astype(F32) + yb[2, chunk].astype(F32))
-        if k:
-            z_out[k - 1] = part.astype(BF16)
-            send(z_out.at[k - 1], zb.at[k - 1], ss.at[13], rs.at[13], zpeer(k))
+    for h in range(PARTS):
+        wait(yb.at[h], xs.at[12 + h])
+        part = (y_mine[h] + yb[h, 0].astype(F32)) + (yb[h, 1].astype(F32) + yb[h, 2].astype(F32))
+        for i in range(CHUNKS):
+            own = part[16 * i:16 * (i + 1)]
+            k = (Z_ORDER + (0,))[CHUNKS * h + i]
+            if k:
+                z_out[k - 1] = own.astype(BF16)
+                send(z_out.at[k - 1], zb.at[k - 1], ss.at[13], rs.at[13], zpeer(k))
     sent.append((zb, ss.at[13]))
     wait(zb, rs.at[13])
-    own = part + jnp.sum(zb[...].astype(F32), axis=0)
+    own = own + jnp.sum(zb[...].astype(F32), axis=0)
 
     def cell(i, j):
-        return xr.at[rows16(i), block(j, 256)]
-
-    xr[rows16(z), block(y, 256)] = own.astype(BF16)
+        return xr.at[block(i, 16), block(j, 256)]
+
+    xr[block(z, 16), block(y, 256)] = own.astype(BF16)
     for k in Z_ORDER:
         send(cell(z, y), cell(z, y), ss.at[14], zs.at[16 + k], zpeer(k))
     sent.append((xr.at[pl.ds(0, 112), pl.ds(0, 256)], ss.at[14]))
@@ -338,12 +337,13 @@
         vmem((2, 1, W), jnp.int32),
         vmem((ITERS, COLS, 1, W), F32),
         vmem((ITERS, ROWS, 1, W), F32),
-        vmem((X, 128, W), BF16),
-        vmem((X - 1, 128, W), BF16),
-        vmem((2 * X, 128, W), BF16),
-        vmem((Y - 1, 128, 256), BF16),
-        vmem((Y - 1, 128, 256), BF16),
-        vmem((128, 256), F32),
+        vmem((PARTS, X * ROWS_IN, W), BF16),
+        vmem((PARTS, X * ROWS_IN, W), BF16),
+        vmem((PARTS, X - 1, ROWS_IN, W), BF16),
+        vmem((PARTS, X - 1, ROWS_IN, W), BF16),
+        vmem((PARTS, Y - 1, ROWS_IN, 256), BF16),
+        vmem((PARTS, Y - 1, ROWS_IN, 256), BF16),
+        vmem((PARTS, ROWS_IN, 256), F32),
         vmem((Z - 1, 16, 256), BF16),
         vmem((Z - 1, 16, 256), BF16),
         vmem((128, D), BF16),
@@ -354,7 +354,7 @@
         vmem((ROWS, 4, D + 128), F32),
         pltpu.SemaphoreType.DMA((5,)),
         pltpu.SemaphoreType.DMA((40,)),
-        pltpu.SemaphoreType.DMA((8,)),
+        pltpu.SemaphoreType.DMA((16,)),
         pltpu.SemaphoreType.DMA((18,)),
         pltpu.SemaphoreType.DMA((18,)),
     ]

time: 86.4 us -> 82.1 us (0.950)
  Pallas kernels: 84.9 us -> 80.5 us
    pallas_call x1, Pallas kernels: 84.9 us -> 80.5 us  [shards(): pl.pallas_call(body, out_shape=jax.ShapeDtypeStruct((4, D), F32), in_spec...]
where the time goes in v4:
time: 82.1 us; the launch traced here: 81.9 us
  Pallas kernels  80.5 us (98%)
  local copies, waits for them, and re-layouts  1.32 us (2%)
    pallas_call x1, Pallas kernels, shards(): pl.pallas_call(body, out_shape=jax.ShapeDtypeStruct((4, D), F32), in_spec...  80.5 us

profile of v4, /device:TPU:1, one launch (start us, length us, event | category | flops | bytes accessed | tf_op | source)
XLA Modules:
  0.0 81.9 jit_solution(2839362901942669634)
XLA Ops:
  0.0 80.5 %procrustes.1 = f32[4,1024]{1,0:T(4,128)} custom-call(bf16[32,512]{1,0:T(8,128)(2,1)} %bitcast.3, bf16[512,128]{1,0:T(8,128)(2,1)} %tgt_hbm.1, bf16[1024,1024]{1,0:T(8,128)(2,1)} %rot_hbm.1, s32[1,512]{1,0:T(1,128)} %bitcast.4, s32[1,512]{1,0:T(1,128)} %bitcast.5), custom_call_target="tpu_custom_call" | custom-call | tf_op jit(solution)/shard_map/procrustes/pallas_call | solution.py:363
  80.6 1.3 %copy.7 = f32[4,1024]{1,0:T(4,128)} copy(f32[4,1024]{1,0:T(4,128)} %procrustes.1) | data formatting | bytes 32768

commit v5 on v4

--- a/solution.py
+++ b/solution.py
@@ -30,7 +30,7 @@
 ROW_ORDER = [d[:2] for d in PLANE_ORDER if d[2] == 0]
 Z_ORDER = (4, 3, 5, 2, 6, 1, 7)
 Z_NEAR = (0, 1, 7, 2, 6, 3, 5, 4)
-PARTS = 2
+PARTS = 4
 ROWS_IN = 128 // PARTS
 CHUNKS = Z // PARTS
 XY_ORDER = (2, 1, 3)
@@ -53,13 +53,19 @@
     pltpu.make_async_copy(ref, ref, sem).wait()
 
 
+def add_up(parts):
+    while len(parts) > 1:
+        parts = [a + b for a, b in zip(parts[::2], parts[1::2])]
+    return parts[0]
+
+
 def block(i, size):
     return pl.ds(pl.multiple_of(i * size, size), size)
 
 
 def body(src_hbm, tgt_hbm, rot_hbm, src_ids, tgt_ids, out_ref,
-         src_t, ordered, tgt, rot, u, kt, ids, colbuf, rowbuf,
-         a_mate, a_out, a_x, x_out, yb, y_out, y_mine, zb, z_out, xr, own4, req, rows, c_out, c_in,
+         src_t, ordered, tgt, rot, u, kt, kst, ids, colbuf, rowbuf,
+         a_mate, a_out, a_x, x_out, yb, y_out, y_mine, zb, z_out, xr, own4, req, rows, stack, squares, c_out, c_in,
          local, zs, xs, ss, rs):
     sent = []
 
@@ -182,10 +188,10 @@
 
     row8 = lax.broadcasted_iota(jnp.int32, (8, W), 0)
 
-    def matvec(v, dims):
+    def matvec(v, matrix):
         high = v.astype(BF16).astype(F32)
         both = jnp.where(row8 == 0, high, jnp.where(row8 == 1, v - high, 0.0)).astype(BF16)
-        return jnp.sum(dot(both, kt[...], dims), axis=0, keepdims=True)
+        return jnp.sum(dot(both, matrix[...], NN), axis=0, keepdims=True)
 
     def meanwhile():
         at = lax.broadcasted_iota(jnp.int32, (128, 128), 0)
@@ -194,6 +200,7 @@
             step = jnp.where(at // 16 == i, k, step)
         to = 32 * (at // 4 % 4) + 4 * ((z + step) % Z) + at % 4
         order = (lax.broadcasted_iota(jnp.int32, (128, 128), 1) == to).astype(BF16)
+        kst[...] = jnp.transpose(kt[...])
         for i in range(ROWS):
             natural = [src_t[128 * j + 32 * (i // 2):128 * j + 32 * (i // 2) + 32]
                        for j in range(4 * (i % 2), 4 * (i % 2) + 4)]
@@ -208,7 +215,7 @@
         if it == 0:
             meanwhile()
         wait(colbuf.at[it, pl.ds(0, COLS - 1)], rs.at[4 + it])
-        return jnp.sum(colbuf[it], axis=0)
+        return add_up([colbuf[it, i] for i in range(COLS)])
 
     def start_row(part, it):
         rowbuf[it, r] = part
@@ -218,15 +225,15 @@
 
     def end_row(it):
         wait(rowbuf.at[it, pl.ds(0, ROWS - 1)], rs.at[7 + it])
-        return jnp.sum(rowbuf[it], axis=0)
+        return add_up([rowbuf[it, i] for i in range(ROWS)])
 
     src_mass = lax.rsqrt(1000.0 + ids[0].astype(F32))
     tgt_mass = lax.rsqrt(1000.0 + ids[1].astype(F32))
     tgt_scale = jnp.ones((1, W), F32)
     for it in range(ITERS):
-        src_scale = src_mass / sum_col(matvec(tgt_scale, NN), it)
+        src_scale = src_mass / sum_col(matvec(tgt_scale, kt), it)
         if it < ITERS - 1:
-            start_row(matvec(src_scale, NT), it)
+            start_row(matvec(src_scale, kst), it)
             tgt_scale = tgt_mass / end_row(it)
 
     plan = (kt[...].astype(F32) * (src_scale * sscale)).astype(BF16)
@@ -238,7 +245,7 @@
         a_out[h] = dot(some_rows(1 - core, h), plan, NT).astype(BF16)
         send(a_out.at[h], a_mate.at[h], ss.at[10], xs.at[4 + h], mate)
     sent.append((a_mate, ss.at[10]))
-    start_row(matvec(src_scale, NT), ITERS - 1)
+    start_row(matvec(src_scale, kst), ITERS - 1)
     tscale_l = jnp.transpose(jnp.broadcast_to(tscale, (W, 128)))[0:1, :]
     kept = []
     for h in range(PARTS):
@@ -281,14 +288,14 @@
     for k in Z_ORDER:
         send(cell(z, y), cell(z, y), ss.at[14], zs.at[16 + k], zpeer(k))
     sent.append((xr.at[pl.ds(0, 112), pl.ds(0, 256)], ss.at[14]))
+    for j in XY_ORDER:
+        send(cell(z, y), cell(z, y), ss.at[16], rs.at[16], ypeer(j))
     for j in range(Y):
         own4[j] = own[4 * j:4 * (j + 1)]
     for d in PLANE_ORDER:
         send(own4.at[(y + d[2]) % Y], req.at[Y * r + y], ss.at[15], rs.at[15], planepeer(d))
     sent.append((req.at[pl.ds(0, ROWS * Y - 1)], ss.at[15]))
     req[Y * r + y] = own4[y]
-    for j in XY_ORDER:
-        send(cell(z, y), cell(z, y), ss.at[16], rs.at[16], ypeer(j))
     for k in (1, 7, 2, 6, 3, 5, 4):
         got = cell((z + Z - k) % Z, y)
         wait(got, zs.at[16 + k])
@@ -303,24 +310,31 @@
 
     xv = xr[...].astype(F32)
     square = jnp.sum(jnp.sum(xv * xv, axis=0, keepdims=True), axis=1, keepdims=True)
+    squares[r] = jnp.broadcast_to(square, (1, 128))
+    for d in ROW_ORDER:
+        send(squares.at[r], squares.at[r], ss.at[18], rs.at[18], rowpeer(d))
+    sent.append((squares.at[pl.ds(0, ROWS - 1)], ss.at[18]))
     gram = dot(rows[...].astype(BF16), xr[...], NT) * (1.0 / (square * (1.0 / (128 * D)) + 1e-30))
     cubic = dot(gram.astype(BF16), xr[...], NN)
     for i in range(ROWS):
-        c_out[i, :, 0:D] = cubic[4 * i:4 * (i + 1)]
-        c_out[i, :, D:] = jnp.broadcast_to(square, (4, 128))
+        for j in range(Y):
+            stack[i, 4 * j:4 * (j + 1)] = cubic[4 * i:4 * (i + 1), 256 * j:256 * (j + 1)]
+    c_out[...] = stack[...].astype(BF16)
     for d in ROW_ORDER:
         peer = rowpeer(d)
         send(c_out.at[peer[0]], c_in.at[r], ss.at[17], rs.at[17], peer)
     sent.append((c_in.at[pl.ds(0, ROWS - 1)], ss.at[17]))
     c_in[r] = c_out[r]
     linear = jnp.concatenate([req[Y * r + j] for j in range(Y)], axis=1)
+    wait(squares.at[pl.ds(0, ROWS - 1)], rs.at[18])
+    each = [squares[i][:, 0:1] for i in range(ROWS)]
+    mean = add_up(each) * (1.0 / (D * D)) + 1e-30
+    inverse = 1.0 / (mean * (4.0 * D))
+    scale = lax.rsqrt(mean) * (1.0 / (2.0 * math.sqrt(D)))
     wait(c_in.at[pl.ds(0, ROWS - 1)], rs.at[17])
-    squares = [c_in[i, 0:1, D:D + 1] for i in range(ROWS)]
-    mean = sum(squares) * (1.0 / (D * D)) + 1e-30
-    inverse = 1.0 / (mean * (4.0 * D))
-    cubic = sum(
-        c_in[i, :, 0:D] * ((squares[i] * (1.0 / (128 * D)) + 1e-30) * inverse) for i in range(ROWS))
-    scale = lax.rsqrt(mean) * (1.0 / (2.0 * math.sqrt(D)))
+    cubic = add_up([
+        c_in[i].astype(F32) * ((each[i] * (1.0 / (128 * D)) + 1e-30) * inverse) for i in range(ROWS)])
+    cubic = jnp.concatenate([cubic[4 * j:4 * (j + 1)] for j in range(Y)], axis=1)
     out_ref[...] = (math.sqrt(D) * scale) * (1.5 * linear - 0.5 * cubic)
     finish()
 
@@ -333,6 +347,7 @@
         vmem((W, D), BF16),
         vmem((D, D), BF16),
         vmem((W, D), BF16),
+        vmem((W, W), BF16),
         vmem((W, W), BF16),
         vmem((2, 1, W), jnp.int32),
         vmem((ITERS, COLS, 1, W), F32),
@@ -350,24 +365,26 @@
         vmem((Y, 4, 256), F32),
         vmem((ROWS * Y, 4, 256), F32),
         vmem((32, D), F32),
-        vmem((ROWS, 4, D + 128), F32),
-        vmem((ROWS, 4, D + 128), F32),
+        vmem((ROWS, 16, 256), F32),
+        vmem((ROWS, 1, 128), F32),
+        vmem((ROWS, 16, 256), BF16),
+        vmem((ROWS, 16, 256), BF16),
         pltpu.SemaphoreType.DMA((5,)),
         pltpu.SemaphoreType.DMA((40,)),
         pltpu.SemaphoreType.DMA((16,)),
-        pltpu.SemaphoreType.DMA((18,)),
-        pltpu.SemaphoreType.DMA((18,)),
+        pltpu.SemaphoreType.DMA((19,)),
+        pltpu.SemaphoreType.DMA((19,)),
     ]
     hbm = pl.BlockSpec(memory_space=pltpu.HBM)
     here = pl.BlockSpec(memory_space=pltpu.VMEM)
     return pl.pallas_call(
         body,
-        out_shape=jax.ShapeDtypeStruct((4, D), F32),
+        out_shape=pltpu.VMEM((4, D), F32),
         in_specs=[hbm] * 5,
         out_specs=here,
         scratch_shapes=scratch,
         compiler_params=pltpu.CompilerParams(
-            collective_id=0, has_side_effects=True, vmem_limit_bytes=63 * 2**20
+            collective_id=0, has_side_effects=True, vmem_limit_bytes=60 * 2**20
         ),
         name="procrustes",
     )(src_emb.T, tgt_emb, rotation, src_ids.reshape(1, W), tgt_ids.reshape(1, W))

time: 82.1 us -> 79.9 us (0.973)
  Pallas kernels: 80.5 us -> 79.2 us
    pallas_call x1, Pallas kernels: 80.5 us -> 79.2 us  [shards(): pl.pallas_call(body, out_shape=pltpu.VMEM((4, D), F32), in_specs=[hbm] *...]
where the time goes in v5:
time: 79.9 us; the launch traced here: 79.8 us
  Pallas kernels  79.2 us (99%)
    pallas_call x1, Pallas kernels, shards(): pl.pallas_call(body, out_shape=pltpu.VMEM((4, D), F32), in_specs=[hbm] *...  79.2 us

profile of v5, /device:TPU:1, one launch (start us, length us, event | category | flops | bytes accessed | tf_op | source)
XLA Modules:
  0.0 79.8 jit_solution(16513233763568002464)
XLA Ops:
  0.0 79.2 %procrustes.1 = f32[4,1024]{1,0:T(4,128)S(1)} custom-call(bf16[32,512]{1,0:T(8,128)(2,1)} %bitcast.3, bf16[512,128]{1,0:T(8,128)(2,1)} %tgt_hbm.1, bf16[1024,1024]{1,0:T(8,128)(2,1)} %rot_hbm.1, s32[1,512]{1,0:T(1,128)} %bitcast.4, s32[1,512]{1,0:T(1,128)} %bitcast.5), custom_call_target="tpu_custom_call" | custom-call | tf_op jit(solution)/shard_map/procrustes/pallas_call | solution.py:380
  79.2 0.6 copy.7

commit v6 on v5

--- a/solution.py
+++ b/solution.py
@@ -29,7 +29,7 @@
     key=lambda d: -2 * hops(d[0], X) - 3 * d[1] - 2 * hops(d[2], Y))
 ROW_ORDER = [d[:2] for d in PLANE_ORDER if d[2] == 0]
 Z_ORDER = (4, 3, 5, 2, 6, 1, 7)
-Z_NEAR = (0, 1, 7, 2, 6, 3, 5, 4)
+Z_NEAR = (0, 2, 6, 1, 7, 3, 5, 4)
 PARTS = 4
 ROWS_IN = 128 // PARTS
 CHUNKS = Z // PARTS
@@ -65,7 +65,7 @@
 
 def body(src_hbm, tgt_hbm, rot_hbm, src_ids, tgt_ids, out_ref,
          src_t, ordered, tgt, rot, u, kt, kst, ids, colbuf, rowbuf,
-         a_mate, a_out, a_x, x_out, yb, y_out, y_mine, zb, z_out, xr, own4, req, rows, stack, squares, c_out, c_in,
+         kt_mate, ord_mate, src_factor, plan, a_x, x_out, yb, y_out, y_mine, zb, z_out, xr, own4, req, rows, stack, squares, c_out, c_in,
          local, zs, xs, ss, rs):
     sent = []
 
@@ -114,7 +114,7 @@
         load.start()
     bar = pltpu.get_barrier_semaphore()
 
-    near = [zpeer(k) for k in Z_ORDER] + [xpeer(k) for k in XY_ORDER] + [ypeer(k) for k in XY_ORDER] + [mate]
+    near = [zpeer(k) for k in (2, 6, 1, 7)] + [xpeer(k) for k in XY_ORDER] + [ypeer(k) for k in XY_ORDER] + [mate]
     for device in near:
         pl.semaphore_signal(bar, inc=1, device_id=device, device_id_type=MESH)
     load_src.wait()
@@ -124,6 +124,10 @@
     def over_y(k):
         got = src_t.at[feature((z + Z - k) % Z, y)]
         wait(mine, zs.at[k])
+        if k in (2, 6):
+            send(got, got, ss.at[0], zs.at[3 if k == 2 else 5], zpeer(1 if k == 2 else 7))
+            half = src_t.at[feature((z + Z - k) % Z, y), pl.ds(0 if k == 2 else W // 2, W // 2)]
+            send(half, half, ss.at[0], zs.at[4], zpeer(k))
         for j in (1, 3, 2):
             send(got, got, ss.at[2], zs.at[32 + k], ypeer(j))
 
@@ -135,7 +139,7 @@
 
     for j in (1, 3, 2):
         send(mine, mine, ss.at[2], zs.at[24 + j], ypeer(j))
-    for k in (2, 6, 3, 5, 4, 1, 7):
+    for k in (2, 6, 1, 7):
         send(mine, mine, ss.at[0], zs.at[k], zpeer(k))
     for k in (1, 3, 2):
         send(my_tgt, my_tgt, ss.at[1], xs.at[k], xpeer(k))
@@ -150,17 +154,17 @@
         wait(got, xs.at[k])
         send(got, got, ss.at[3], rs.at[3], mate)
 
+    over_y(2)
+    over_y(6)
     over_z(1)
     over_z(3)
-    over_y(2)
-    over_y(6)
     over_z(2)
+    over_y(3)
+    over_y(5)
     forward_tgt(1)
     forward_tgt(3)
-    over_y(3)
-    over_y(5)
+    over_y(4)
     forward_tgt(2)
-    over_y(4)
 
     wait(tgt.at[:, pl.ds(0, 512)], rs.at[3])
     wait(rot, local.at[2])
@@ -205,6 +209,9 @@
             natural = [src_t[128 * j + 32 * (i // 2):128 * j + 32 * (i // 2) + 32]
                        for j in range(4 * (i % 2), 4 * (i % 2) + 4)]
             ordered[i] = dot(order, jnp.concatenate(natural, axis=0), NN).astype(BF16)
+        for j in range(X):
+            send(ordered.at[2 * j + (1 - core)], ord_mate.at[j], ss.at[19], xs.at[5], mate)
+        sent.append((ord_mate, ss.at[19]))
 
     def sum_col(part, it):
         colbuf[it, c] = part
@@ -213,8 +220,13 @@
             send(colbuf.at[it, c], colbuf.at[it, c], ss.at[4 + it], rs.at[4 + it], colpeer(d))
         sent.append((colbuf.at[it, pl.ds(0, COLS - 1)], ss.at[4 + it]))
         if it == 0:
+            send(kt, kt_mate, ss.at[10], xs.at[4], mate)
+            sent.append((kt_mate, ss.at[10]))
             meanwhile()
         wait(colbuf.at[it, pl.ds(0, COLS - 1)], rs.at[4 + it])
+        if it == 0:
+            wait(kt_mate, xs.at[4])
+            wait(ord_mate, xs.at[5])
         return add_up([colbuf[it, i] for i in range(COLS)])
 
     def start_row(part, it):
@@ -236,40 +248,42 @@
             start_row(matvec(src_scale, kst), it)
             tgt_scale = tgt_mass / end_row(it)
 
-    plan = (kt[...].astype(F32) * (src_scale * sscale)).astype(BF16)
-    def some_rows(k, h):
+    src_factor[0] = src_scale * sscale
+    send(src_factor.at[0], src_factor.at[1], ss.at[20], xs.at[6], mate)
+    sent.append((src_factor.at[0], ss.at[20]))
+    plan[0] = (kt[...].astype(F32) * src_factor[0]).astype(BF16)
+
+    def some_rows(h, i):
         first = pl.ds(ROWS_IN * h, ROWS_IN)
-        return jnp.concatenate([ordered[2 * ((x + j) % X) + k, first] for j in range(X)], axis=0)
-
-    for h in range(PARTS):
-        a_out[h] = dot(some_rows(1 - core, h), plan, NT).astype(BF16)
-        send(a_out.at[h], a_mate.at[h], ss.at[10], xs.at[4 + h], mate)
-    sent.append((a_mate, ss.at[10]))
+        rows_of = [ordered[2 * ((x + j) % X) + core, first] if i == 0 else ord_mate[(x + j) % X, first] for j in range(X)]
+        return dot(jnp.concatenate(rows_of, axis=0), plan[i], NT)
+
+    first_part = some_rows(0, 0)
     start_row(matvec(src_scale, kst), ITERS - 1)
     tscale_l = jnp.transpose(jnp.broadcast_to(tscale, (W, 128)))[0:1, :]
+    wait(src_factor.at[1], xs.at[6])
+    plan[1] = (kt_mate[...].astype(F32) * src_factor[1]).astype(BF16)
     kept = []
     for h in range(PARTS):
-        half = dot(some_rows(core, h), plan, NT)
-        wait(a_mate.at[h], xs.at[4 + h])
-        half = half + a_mate[h].astype(F32)
-        kept.append(half[0:ROWS_IN])
+        part = (some_rows(h, 0) if h else first_part) + some_rows(h, 1)
+        kept.append(part[0:ROWS_IN])
         for k in (2, 1, 3):
-            x_out[h, k - 1] = half[ROWS_IN * k:ROWS_IN * (k + 1)].astype(BF16)
-            send(x_out.at[h, k - 1], a_x.at[h, k - 1], ss.at[11], xs.at[8 + h], xpeer(k))
+            x_out[h, k - 1] = part[ROWS_IN * k:ROWS_IN * (k + 1)].astype(BF16)
+            send(x_out.at[h, k - 1], a_x.at[h, k - 1], ss.at[11], xs.at[12 + h], xpeer(k))
     sent.append((a_x, ss.at[11]))
     factor = (tgt_mass / end_row(ITERS - 1)) * tscale_l
 
     for h in range(PARTS):
-        wait(a_x.at[h], xs.at[8 + h])
+        wait(a_x.at[h], xs.at[12 + h])
         total = kept[h] + ((a_x[h, 0].astype(F32) + a_x[h, 1].astype(F32)) + a_x[h, 2].astype(F32))
         total = (total * factor).astype(BF16)
         for j in XY_ORDER:
             y_out[h, j - 1] = dot(total, tgt[:, block((y + j) % Y, 256)], NN).astype(BF16)
-            send(y_out.at[h, j - 1], yb.at[h, j - 1], ss.at[12], xs.at[12 + h], ypeer(j))
+            send(y_out.at[h, j - 1], yb.at[h, j - 1], ss.at[12], xs.at[20 + h], ypeer(j))
         y_mine[h] = dot(total, tgt[:, block(y, 256)], NN)
     sent.append((yb, ss.at[12]))
     for h in range(PARTS):
-        wait(yb.at[h], xs.at[12 + h])
+        wait(yb.at[h], xs.at[20 + h])
         part = (y_mine[h] + yb[h, 0].astype(F32)) + (yb[h, 1].astype(F32) + yb[h, 2].astype(F32))
         for i in range(CHUNKS):
             own = part[16 * i:16 * (i + 1)]
@@ -352,8 +366,10 @@
         vmem((2, 1, W), jnp.int32),
         vmem((ITERS, COLS, 1, W), F32),
         vmem((ITERS, ROWS, 1, W), F32),
-        vmem((PARTS, X * ROWS_IN, W), BF16),
-        vmem((PARTS, X * ROWS_IN, W), BF16),
+        vmem((W, W), BF16),
+        vmem((X, 128, W), BF16),
+        vmem((2, 1, W), F32),
+        vmem((2, W, W), BF16),
         vmem((PARTS, X - 1, ROWS_IN, W), BF16),
         vmem((PARTS, X - 1, ROWS_IN, W), BF16),
         vmem((PARTS, Y - 1, ROWS_IN, 256), BF16),
@@ -371,9 +387,9 @@
         vmem((ROWS, 16, 256), BF16),
         pltpu.SemaphoreType.DMA((5,)),
         pltpu.SemaphoreType.DMA((40,)),
-        pltpu.SemaphoreType.DMA((16,)),
-        pltpu.SemaphoreType.DMA((19,)),
-        pltpu.SemaphoreType.DMA((19,)),
+        pltpu.SemaphoreType.DMA((28,)),
+        pltpu.SemaphoreType.DMA((21,)),
+        pltpu.SemaphoreType.DMA((21,)),
     ]
     hbm = pl.BlockSpec(memory_space=pltpu.HBM)
     here = pl.BlockSpec(memory_space=pltpu.VMEM)

time: 79.9 us -> 77.5 us (0.970)
  Pallas kernels: 79.2 us -> 76.8 us
    pallas_call x1, Pallas kernels: 79.2 us -> 76.8 us  [shards(): pl.pallas_call(body, out_shape=pltpu.VMEM((4, D), F32), in_specs=[hbm] *...]
where the time goes in v6:
time: 77.5 us; the launch traced here: 77.4 us
  Pallas kernels  76.8 us (99%)
    pallas_call x1, Pallas kernels, shards(): pl.pallas_call(body, out_shape=pltpu.VMEM((4, D), F32), in_specs=[hbm] *...  76.8 us

profile of v6, /device:TPU:1, one launch (start us, length us, event | category | flops | bytes accessed | tf_op | source)
XLA Modules:
  0.0 77.4 jit_solution(3570714974717110914)
XLA Ops:
  0.0 76.8 %procrustes.1 = f32[4,1024]{1,0:T(4,128)S(1)} custom-call(bf16[32,512]{1,0:T(8,128)(2,1)} %bitcast.3, bf16[512,128]{1,0:T(8,128)(2,1)} %tgt_hbm.1, bf16[1024,1024]{1,0:T(8,128)(2,1)} %rot_hbm.1, s32[1,512]{1,0:T(1,128)} %bitcast.4, s32[1,512]{1,0:T(1,128)} %bitcast.5), custom_call_target="tpu_custom_call" | custom-call | tf_op jit(solution)/shard_map/procrustes/pallas_call | solution.py:396
  76.8 0.6 copy.7

commit v7 on v6

--- a/solution.py
+++ b/solution.py
@@ -65,7 +65,7 @@
 
 def body(src_hbm, tgt_hbm, rot_hbm, src_ids, tgt_ids, out_ref,
          src_t, ordered, tgt, rot, u, kt, kst, ids, colbuf, rowbuf,
-         kt_mate, ord_mate, src_factor, plan, a_x, x_out, yb, y_out, y_mine, zb, z_out, xr, own4, req, rows, stack, squares, c_out, c_in,
+         kt_mate, ord_mate, src_factor, tscale_row, plan, a_x, x_out, yb, y_out, y_mine, zb, z_out, xr, own4, req, rows, stack, squares, c_out, c_in,
          local, zs, xs, ss, rs):
     sent = []
 
@@ -204,7 +204,6 @@
             step = jnp.where(at // 16 == i, k, step)
         to = 32 * (at // 4 % 4) + 4 * ((z + step) % Z) + at % 4
         order = (lax.broadcasted_iota(jnp.int32, (128, 128), 1) == to).astype(BF16)
-        kst[...] = jnp.transpose(kt[...])
         for i in range(ROWS):
             natural = [src_t[128 * j + 32 * (i // 2):128 * j + 32 * (i // 2) + 32]
                        for j in range(4 * (i % 2), 4 * (i % 2) + 4)]
@@ -222,11 +221,11 @@
         if it == 0:
             send(kt, kt_mate, ss.at[10], xs.at[4], mate)
             sent.append((kt_mate, ss.at[10]))
+            kst[...] = jnp.transpose(kt[...])
+            tscale_row[...] = jnp.transpose(jnp.broadcast_to(tscale, (W, 128)))[0:1, :]
+        elif it == 1:
             meanwhile()
         wait(colbuf.at[it, pl.ds(0, COLS - 1)], rs.at[4 + it])
-        if it == 0:
-            wait(kt_mate, xs.at[4])
-            wait(ord_mate, xs.at[5])
         return add_up([colbuf[it, i] for i in range(COLS)])
 
     def start_row(part, it):
@@ -248,6 +247,8 @@
             start_row(matvec(src_scale, kst), it)
             tgt_scale = tgt_mass / end_row(it)
 
+    wait(kt_mate, xs.at[4])
+    wait(ord_mate, xs.at[5])
     src_factor[0] = src_scale * sscale
     send(src_factor.at[0], src_factor.at[1], ss.at[20], xs.at[6], mate)
     sent.append((src_factor.at[0], ss.at[20]))
@@ -259,8 +260,6 @@
         return dot(jnp.concatenate(rows_of, axis=0), plan[i], NT)
 
     first_part = some_rows(0, 0)
-    start_row(matvec(src_scale, kst), ITERS - 1)
-    tscale_l = jnp.transpose(jnp.broadcast_to(tscale, (W, 128)))[0:1, :]
     wait(src_factor.at[1], xs.at[6])
     plan[1] = (kt_mate[...].astype(F32) * src_factor[1]).astype(BF16)
     kept = []
@@ -270,8 +269,10 @@
         for k in (2, 1, 3):
             x_out[h, k - 1] = part[ROWS_IN * k:ROWS_IN * (k + 1)].astype(BF16)
             send(x_out.at[h, k - 1], a_x.at[h, k - 1], ss.at[11], xs.at[12 + h], xpeer(k))
+        if h == 0:
+            start_row(matvec(src_scale, kst), ITERS - 1)
     sent.append((a_x, ss.at[11]))
-    factor = (tgt_mass / end_row(ITERS - 1)) * tscale_l
+    factor = (tgt_mass / end_row(ITERS - 1)) * tscale_row[...]
 
     for h in range(PARTS):
         wait(a_x.at[h], xs.at[12 + h])
@@ -325,6 +326,8 @@
     xv = xr[...].astype(F32)
     square = jnp.sum(jnp.sum(xv * xv, axis=0, keepdims=True), axis=1, keepdims=True)
     squares[r] = jnp.broadcast_to(square, (1, 128))
+    earlier = list(sent)
+    sent.clear()
     for d in ROW_ORDER:
         send(squares.at[r], squares.at[r], ss.at[18], rs.at[18], rowpeer(d))
     sent.append((squares.at[pl.ds(0, ROWS - 1)], ss.at[18]))
@@ -339,6 +342,8 @@
         send(c_out.at[peer[0]], c_in.at[r], ss.at[17], rs.at[17], peer)
     sent.append((c_in.at[pl.ds(0, ROWS - 1)], ss.at[17]))
     c_in[r] = c_out[r]
+    for ref, sem in earlier:
+        wait(ref, sem)
     linear = jnp.concatenate([req[Y * r + j] for j in range(Y)], axis=1)
     wait(squares.at[pl.ds(0, ROWS - 1)], rs.at[18])
     each = [squares[i][:, 0:1] for i in range(ROWS)]
@@ -369,6 +374,7 @@
         vmem((W, W), BF16),
         vmem((X, 128, W), BF16),
         vmem((2, 1, W), F32),
+        vmem((1, W), F32),
         vmem((2, W, W), BF16),
         vmem((PARTS, X - 1, ROWS_IN, W), BF16),
         vmem((PARTS, X - 1, ROWS_IN, W), BF16),

time: 77.5 us -> 77.5 us (level)
  no operation moved by 1% of the time
where the time goes in v7:
time: 77.5 us; the launch traced here: 77.4 us
  Pallas kernels  76.8 us (99%)
    pallas_call x1, Pallas kernels, shards(): pl.pallas_call(body, out_shape=pltpu.VMEM((4, D), F32), in_specs=[hbm] *...  76.8 us

profile of v7, /device:TPU:1, one launch (start us, length us, event | category | flops | bytes accessed | tf_op | source)
XLA Modules:
  0.0 77.4 jit_solution(16089447052780790595)
XLA Ops:
  0.0 76.8 %procrustes.1 = f32[4,1024]{1,0:T(4,128)S(1)} custom-call(bf16[32,512]{1,0:T(8,128)(2,1)} %bitcast.3, bf16[512,128]{1,0:T(8,128)(2,1)} %tgt_hbm.1, bf16[1024,1024]{1,0:T(8,128)(2,1)} %rot_hbm.1, s32[1,512]{1,0:T(1,128)} %bitcast.4, s32[1,512]{1,0:T(1,128)} %bitcast.5), custom_call_target="tpu_custom_call" | custom-call | tf_op jit(solution)/shard_map/procrustes/pallas_call | solution.py:402
  76.8 0.6 copy.7

commit v8 on v7

--- a/solution.py
+++ b/solution.py
@@ -296,46 +296,37 @@
     wait(zb, rs.at[13])
     own = own + jnp.sum(zb[...].astype(F32), axis=0)
 
-    def cell(i, j):
-        return xr.at[block(i, 16), block(j, 256)]
-
-    xr[block(z, 16), block(y, 256)] = own.astype(BF16)
-    for k in Z_ORDER:
-        send(cell(z, y), cell(z, y), ss.at[14], zs.at[16 + k], zpeer(k))
-    sent.append((xr.at[pl.ds(0, 112), pl.ds(0, 256)], ss.at[14]))
-    for j in XY_ORDER:
-        send(cell(z, y), cell(z, y), ss.at[16], rs.at[16], ypeer(j))
+    xr[c] = own.astype(BF16)
+    for d in COL_ORDER:
+        send(xr.at[c], xr.at[c], ss.at[14], rs.at[14], colpeer(d))
+    sent.append((xr.at[pl.ds(0, COLS - 1)], ss.at[14]))
     for j in range(Y):
         own4[j] = own[4 * j:4 * (j + 1)]
     for d in PLANE_ORDER:
         send(own4.at[(y + d[2]) % Y], req.at[Y * r + y], ss.at[15], rs.at[15], planepeer(d))
     sent.append((req.at[pl.ds(0, ROWS * Y - 1)], ss.at[15]))
     req[Y * r + y] = own4[y]
-    for k in (1, 7, 2, 6, 3, 5, 4):
-        got = cell((z + Z - k) % Z, y)
-        wait(got, zs.at[16 + k])
-        for j in XY_ORDER:
-            send(got, got, ss.at[16], rs.at[16], ypeer(j))
-    sent.append((xr.at[pl.ds(0, 96), :], ss.at[16]))
     wait(req.at[pl.ds(0, ROWS * Y - 1)], rs.at[15])
     for i in range(ROWS):
         for j in range(Y):
             rows[4 * i:4 * (i + 1), 256 * j:256 * (j + 1)] = req[Y * i + j]
-    wait(xr.at[pl.ds(0, 96), :], rs.at[16])
-
-    xv = xr[...].astype(F32)
-    square = jnp.sum(jnp.sum(xv * xv, axis=0, keepdims=True), axis=1, keepdims=True)
+    wait(xr.at[pl.ds(0, COLS - 1)], rs.at[14])
+
+    lanes = [xr[Z * j:Z * (j + 1)].reshape(128, 256) for j in range(Y)]
+    square = add_up([jnp.sum(v.astype(F32) * v.astype(F32), axis=0, keepdims=True) for v in lanes])
+    square = jnp.sum(square, axis=1, keepdims=True)
     squares[r] = jnp.broadcast_to(square, (1, 128))
     earlier = list(sent)
     sent.clear()
     for d in ROW_ORDER:
         send(squares.at[r], squares.at[r], ss.at[18], rs.at[18], rowpeer(d))
     sent.append((squares.at[pl.ds(0, ROWS - 1)], ss.at[18]))
-    gram = dot(rows[...].astype(BF16), xr[...], NT) * (1.0 / (square * (1.0 / (128 * D)) + 1e-30))
-    cubic = dot(gram.astype(BF16), xr[...], NN)
-    for i in range(ROWS):
-        for j in range(Y):
-            stack[i, 4 * j:4 * (j + 1)] = cubic[4 * i:4 * (i + 1), 256 * j:256 * (j + 1)]
+    gram = add_up([dot(rows[:, 256 * j:256 * (j + 1)].astype(BF16), lanes[j], NT) for j in range(Y)])
+    gram = (gram * (1.0 / (square * (1.0 / (128 * D)) + 1e-30))).astype(BF16)
+    for j in range(Y):
+        cubic = dot(gram, lanes[j], NN)
+        for i in range(ROWS):
+            stack[i, 4 * j:4 * (j + 1)] = cubic[4 * i:4 * (i + 1)]
     c_out[...] = stack[...].astype(BF16)
     for d in ROW_ORDER:
         peer = rowpeer(d)
@@ -383,7 +374,7 @@
         vmem((PARTS, ROWS_IN, 256), F32),
         vmem((Z - 1, 16, 256), BF16),
         vmem((Z - 1, 16, 256), BF16),
-        vmem((128, D), BF16),
+        vmem((COLS, 16, 256), BF16),
         vmem((Y, 4, 256), F32),
         vmem((ROWS * Y, 4, 256), F32),
         vmem((32, D), F32),

time: 77.5 us -> 77.6 us (level)
  no operation moved by 1% of the time
where the time goes in v8:
time: 77.6 us; the launch traced here: 77.5 us
  Pallas kernels  76.9 us (99%)
    pallas_call x1, Pallas kernels, shards(): pl.pallas_call(body, out_shape=pltpu.VMEM((4, D), F32), in_specs=[hbm] *...  76.9 us

profile of v8, /device:TPU:1, one launch (start us, length us, event | category | flops | bytes accessed | tf_op | source)
XLA Modules:
  0.0 77.5 jit_solution(8382767833601091573)
XLA Ops:
  0.0 76.9 %procrustes.1 = f32[4,1024]{1,0:T(4,128)S(1)} custom-call(bf16[32,512]{1,0:T(8,128)(2,1)} %bitcast.3, bf16[512,128]{1,0:T(8,128)(2,1)} %tgt_hbm.1, bf16[1024,1024]{1,0:T(8,128)(2,1)} %rot_hbm.1, s32[1,512]{1,0:T(1,128)} %bitcast.4, s32[1,512]{1,0:T(1,128)} %bitcast.5), custom_call_target="tpu_custom_call" | custom-call | tf_op jit(solution)/shard_map/procrustes/pallas_call | solution.py:393
  76.9 0.6 copy.7

commit v9 on v8

--- a/solution.py
+++ b/solution.py
@@ -65,7 +65,7 @@
 
 def body(src_hbm, tgt_hbm, rot_hbm, src_ids, tgt_ids, out_ref,
          src_t, ordered, tgt, rot, u, kt, kst, ids, colbuf, rowbuf,
-         kt_mate, ord_mate, src_factor, tscale_row, plan, a_x, x_out, yb, y_out, y_mine, zb, z_out, xr, own4, req, rows, stack, squares, c_out, c_in,
+         kt_mate, ord_mate, src_factor, plan, a_x, x_out, yb, y_out, y_mine, zb, z_out, xr, own4, req, rows, stack, squares, c_out, c_in,
          local, zs, xs, ss, rs):
     sent = []
 
@@ -204,6 +204,7 @@
             step = jnp.where(at // 16 == i, k, step)
         to = 32 * (at // 4 % 4) + 4 * ((z + step) % Z) + at % 4
         order = (lax.broadcasted_iota(jnp.int32, (128, 128), 1) == to).astype(BF16)
+        kst[...] = jnp.transpose(kt[...])
         for i in range(ROWS):
             natural = [src_t[128 * j + 32 * (i // 2):128 * j + 32 * (i // 2) + 32]
                        for j in range(4 * (i % 2), 4 * (i % 2) + 4)]
@@ -221,11 +222,11 @@
         if it == 0:
             send(kt, kt_mate, ss.at[10], xs.at[4], mate)
             sent.append((kt_mate, ss.at[10]))
-            kst[...] = jnp.transpose(kt[...])
-            tscale_row[...] = jnp.transpose(jnp.broadcast_to(tscale, (W, 128)))[0:1, :]
-        elif it == 1:
             meanwhile()
         wait(colbuf.at[it, pl.ds(0, COLS - 1)], rs.at[4 + it])
+        if it == 0:
+            wait(kt_mate, xs.at[4])
+            wait(ord_mate, xs.at[5])
         return add_up([colbuf[it, i] for i in range(COLS)])
 
     def start_row(part, it):
@@ -247,8 +248,6 @@
             start_row(matvec(src_scale, kst), it)
             tgt_scale = tgt_mass / end_row(it)
 
-    wait(kt_mate, xs.at[4])
-    wait(ord_mate, xs.at[5])
     src_factor[0] = src_scale * sscale
     send(src_factor.at[0], src_factor.at[1], ss.at[20], xs.at[6], mate)
     sent.append((src_factor.at[0], ss.at[20]))
@@ -260,6 +259,8 @@
         return dot(jnp.concatenate(rows_of, axis=0), plan[i], NT)
 
     first_part = some_rows(0, 0)
+    start_row(matvec(src_scale, kst), ITERS - 1)
+    tscale_l = jnp.transpose(jnp.broadcast_to(tscale, (W, 128)))[0:1, :]
     wait(src_factor.at[1], xs.at[6])
     plan[1] = (kt_mate[...].astype(F32) * src_factor[1]).astype(BF16)
     kept = []
@@ -269,10 +270,8 @@
         for k in (2, 1, 3):
             x_out[h, k - 1] = part[ROWS_IN * k:ROWS_IN * (k + 1)].astype(BF16)
             send(x_out.at[h, k - 1], a_x.at[h, k - 1], ss.at[11], xs.at[12 + h], xpeer(k))
-        if h == 0:
-            start_row(matvec(src_scale, kst), ITERS - 1)
     sent.append((a_x, ss.at[11]))
-    factor = (tgt_mass / end_row(ITERS - 1)) * tscale_row[...]
+    factor = (tgt_mass / end_row(ITERS - 1)) * tscale_l
 
     for h in range(PARTS):
         wait(a_x.at[h], xs.at[12 + h])
@@ -365,7 +364,6 @@
         vmem((W, W), BF16),
         vmem((X, 128, W), BF16),
         vmem((2, 1, W), F32),
-        vmem((1, W), F32),
         vmem((2, W, W), BF16),
         vmem((PARTS, X - 1, ROWS_IN, W), BF16),
         vmem((PARTS, X - 1, ROWS_IN, W), BF16),

time: 77.6 us -> 77.4 us (level)
  no operation moved by 1% of the time
where the time goes in v9:
time: 77.4 us; the launch traced here: 77.3 us
  Pallas kernels  76.7 us (99%)
    pallas_call x1, Pallas kernels, shards(): pl.pallas_call(body, out_shape=pltpu.VMEM((4, D), F32), in_specs=[hbm] *...  76.7 us

profile of v9, /device:TPU:1, one launch (start us, length us, event | category | flops | bytes accessed | tf_op | source)
XLA Modules:
  0.0 77.3 jit_solution(18187514781379849521)
XLA Ops:
  0.0 76.7 %procrustes.1 = f32[4,1024]{1,0:T(4,128)S(1)} custom-call(bf16[32,512]{1,0:T(8,128)(2,1)} %bitcast.3, bf16[512,128]{1,0:T(8,128)(2,1)} %tgt_hbm.1, bf16[1024,1024]{1,0:T(8,128)(2,1)} %rot_hbm.1, s32[1,512]{1,0:T(1,128)} %bitcast.4, s32[1,512]{1,0:T(1,128)} %bitcast.5), custom_call_target="tpu_custom_call" | custom-call | tf_op jit(solution)/shard_map/procrustes/pallas_call | solution.py:391
  76.7 0.6 copy.7

commit v10 on v6

--- a/solution.py
+++ b/solution.py
@@ -100,23 +100,16 @@
         return pl.ds(pl.multiple_of(128 * i + 32 * j, 32), 32)
 
     mine = src_t.at[feature(z, y)]
+    bar = pltpu.get_barrier_semaphore()
+
+    near = [zpeer(k) for k in (2, 6, 1, 7)] + [xpeer(k) for k in XY_ORDER] + [ypeer(k) for k in XY_ORDER] + [mate]
+    for device in near:
+        pl.semaphore_signal(bar, inc=1, device_id=device, device_id_type=MESH)
     load_src = pltpu.make_async_copy(src_hbm, mine, local.at[0])
     load_src.start()
     my_tgt = tgt.at[:, block(r, 128)]
     load_tgt = pltpu.make_async_copy(tgt_hbm, my_tgt, local.at[1])
     load_tgt.start()
-    for i in range(Z):
-        for j in range(Y):
-            pltpu.make_async_copy(
-                rot_hbm.at[pl.ds(32 * (Z * j + i), 32)], rot.at[pl.ds(128 * i + 32 * j, 32)], local.at[2]).start()
-    load_ids = [pltpu.make_async_copy(ref, ids.at[i], local.at[3 + i]) for i, ref in enumerate((src_ids, tgt_ids))]
-    for load in load_ids:
-        load.start()
-    bar = pltpu.get_barrier_semaphore()
-
-    near = [zpeer(k) for k in (2, 6, 1, 7)] + [xpeer(k) for k in XY_ORDER] + [ypeer(k) for k in XY_ORDER] + [mate]
-    for device in near:
-        pl.semaphore_signal(bar, inc=1, device_id=device, device_id_type=MESH)
     load_src.wait()
     load_tgt.wait()
     pl.semaphore_wait(bar, len(near))
@@ -144,6 +137,13 @@
     for k in (1, 3, 2):
         send(my_tgt, my_tgt, ss.at[1], xs.at[k], xpeer(k))
     send(my_tgt, my_tgt, ss.at[3], rs.at[3], mate)
+    for i in range(Z):
+        for j in range(Y):
+            pltpu.make_async_copy(
+                rot_hbm.at[pl.ds(32 * (Z * j + i), 32)], rot.at[pl.ds(128 * i + 32 * j, 32)], local.at[2]).start()
+    load_ids = [pltpu.make_async_copy(ref, ids.at[i], local.at[3 + i]) for i, ref in enumerate((src_ids, tgt_ids))]
+    for load in load_ids:
+        load.start()
     sent.append((src_t.at[pl.ds(0, 13 * 32), :], ss.at[0]))
     sent.append((tgt.at[:, pl.ds(0, 384)], ss.at[1]))
     sent.append((src_t.at[pl.ds(0, 18 * 32), :], ss.at[2]))

time: 77.5 us -> 77.3 us (level)
  no operation moved by 1% of the time
where the time goes in v10:
time: 77.3 us; the launch traced here: 77.2 us
  Pallas kernels  76.6 us (99%)
    pallas_call x1, Pallas kernels, shards(): pl.pallas_call(body, out_shape=pltpu.VMEM((4, D), F32), in_specs=[hbm] *...  76.6 us

profile of v10, /device:TPU:1, one launch (start us, length us, event | category | flops | bytes accessed | tf_op | source)
XLA Modules:
  0.0 77.2 jit_solution(8918038211569345516)
XLA Ops:
  0.0 76.6 %procrustes.1 = f32[4,1024]{1,0:T(4,128)S(1)} custom-call(bf16[32,512]{1,0:T(8,128)(2,1)} %bitcast.3, bf16[512,128]{1,0:T(8,128)(2,1)} %tgt_hbm.1, bf16[1024,1024]{1,0:T(8,128)(2,1)} %rot_hbm.1, s32[1,512]{1,0:T(1,128)} %bitcast.4, s32[1,512]{1,0:T(1,128)} %bitcast.5), custom_call_target="tpu_custom_call" | custom-call | tf_op jit(solution)/shard_map/procrustes/pallas_call | solution.py:396
  76.6 0.6 copy.7

commit v11 on v6

--- a/solution.py
+++ b/solution.py
@@ -259,7 +259,6 @@
         return dot(jnp.concatenate(rows_of, axis=0), plan[i], NT)
 
     first_part = some_rows(0, 0)
-    start_row(matvec(src_scale, kst), ITERS - 1)
     tscale_l = jnp.transpose(jnp.broadcast_to(tscale, (W, 128)))[0:1, :]
     wait(src_factor.at[1], xs.at[6])
     plan[1] = (kt_mate[...].astype(F32) * src_factor[1]).astype(BF16)
@@ -270,6 +269,8 @@
         for k in (2, 1, 3):
             x_out[h, k - 1] = part[ROWS_IN * k:ROWS_IN * (k + 1)].astype(BF16)
             send(x_out.at[h, k - 1], a_x.at[h, k - 1], ss.at[11], xs.at[12 + h], xpeer(k))
+        if h == 0:
+            start_row(matvec(src_scale, kst), ITERS - 1)
     sent.append((a_x, ss.at[11]))
     factor = (tgt_mass / end_row(ITERS - 1)) * tscale_l
 

time: 77.5 us -> 77.6 us (level)
  no operation moved by 1% of the time
where the time goes in v11:
time: 77.6 us; the launch traced here: 77.5 us
  Pallas kernels  76.9 us (99%)
    pallas_call x1, Pallas kernels, shards(): pl.pallas_call(body, out_shape=pltpu.VMEM((4, D), F32), in_specs=[hbm] *...  76.9 us

profile of v11, /device:TPU:1, one launch (start us, length us, event | category | flops | bytes accessed | tf_op | source)
XLA Modules:
  0.0 77.5 jit_solution(13667152903476784077)
XLA Ops:
  0.0 76.9 %procrustes.1 = f32[4,1024]{1,0:T(4,128)S(1)} custom-call(bf16[32,512]{1,0:T(8,128)(2,1)} %bitcast.3, bf16[512,128]{1,0:T(8,128)(2,1)} %tgt_hbm.1, bf16[1024,1024]{1,0:T(8,128)(2,1)} %rot_hbm.1, s32[1,512]{1,0:T(1,128)} %bitcast.4, s32[1,512]{1,0:T(1,128)} %bitcast.5), custom_call_target="tpu_custom_call" | custom-call | tf_op jit(solution)/shard_map/procrustes/pallas_call | solution.py:397
  76.9 0.6 copy.7
